TPU v7x, 128 devices: a whole 4x4x4 slice. The times are simulated.
128 devices in a mesh: row: 2 (over y_hi), inst: 4 (over x), mesh: 16 (over y_lo, z, core).
Axes of the slice: x: 4, y: 4 (y_hi: 2, y_lo: 2; y = y_hi * 2 + y_lo), z: 4, core: 2. Of those that a mesh axis runs over, the one named last changes fastest.
Arguments:
- state: float32 [2, 8, 6, 128, 64, 128], P('row', 'inst', None, 'mesh'), may hold values from -6 to 6
- viscosity: float32 [2, 128, 64, 128], P('row', 'mesh'), may hold values from 0.05 to 0.5
- blade_counts: int32 [2], replicated, may hold values from 20 to 79
- mode_orders: int32 [8], replicated, may hold values from 1 to 63
Outputs:
- new_state: float32 [2, 8, 6, 128, 64, 128], P('row', 'inst', None, 'mesh')
- residual: float32 [2, 8, 6, 128, 64, 128], P('row', 'inst', None, 'mesh')
All inputs are finite; a program needn't handle non-finite values.
Results may differ from a plain program's by a relative error of at most 0.0001.
Values sent between devices are 32-bit elements; how exact they have to be, the bound alone decides.
No kernel may reach another device: no remote copies, remote signals or barrier semaphores. Data moves between devices by JAX's collectives and lax.ppermute only.
A program may use at most 128 MiB of HBM per device.

v0:
```python
import functools
import math

import numpy as np

import jax
import jax.numpy as jnp
from jax import lax
from jax.experimental import pallas as pl
from jax.experimental.pallas import tpu as pltpu
from jax.sharding import PartitionSpec as P

INST = 8
OUTER = 6
MODES = 24
LIMIT = 14 * 1024 * 1024
VMEM = pl.BlockSpec(memory_space=pltpu.VMEM)
SMEM = pl.BlockSpec(memory_space=pltpu.SMEM)
ANY = pl.BlockSpec(memory_space=pl.ANY)
HBM = pl.BlockSpec(memory_space=pltpu.HBM)
D1 = -0.5 / math.tan(math.pi / 8)
D2 = 0.5 / math.tan(math.pi / 4)
D3 = -0.5 / math.tan(3 * math.pi / 8)


def shaped(*dims):
    return jax.ShapeDtypeStruct(dims, jnp.float32)


def cost():
    return pl.CostEstimate(flops=1, bytes_accessed=1, transcendentals=0)


def inverse_parts(length):
    steps = np.arange(1, length + 1).astype(np.float64)
    basis = math.sqrt(2.0 / (length + 1)) * np.sin(
        math.pi * steps[:, None] * steps[None, :] / (length + 1)
    )
    eigen = 2.0 - np.cos(math.pi * steps / (length + 1))
    inverse = (0.2 * (basis / eigen[None, :]) @ basis.T).astype(np.float32)
    high = inverse.astype(jnp.bfloat16)
    low = (inverse - high.astype(np.float32)).astype(jnp.bfloat16)
    return np.concatenate([high, low, high], axis=1)


def split_bf16(x):
    high = x.astype(jnp.bfloat16)
    return high, (x - high.astype(jnp.float32)).astype(jnp.bfloat16)


def params():
    return pltpu.CompilerParams(vmem_limit_bytes=LIMIT)


def pack_kernel(planes, field, *rest):
    sems = rest[-1]
    copies = []

    def copy(source, target):
        one = pltpu.make_async_copy(source, target, sems.at[len(copies)])
        one.start()
        copies.append(one)

    outs = rest[:3]
    for k, out in zip((1, 3, 2), outs):
        place = lax.rem(lax.axis_index("inst") + k, 4) * 16
        rows = pl.ds(pl.multiple_of(place, 16), 16)
        done = 0
        for start, size in planes:
            for b in range(0, field.shape[0], 4):
                copy(
                    field.at[b : b + 4, start : start + size, rows, :],
                    out.at[b : b + 4, done : done + size],
                )
            done += size
    for one in copies:
        one.wait()


def edges_kernel(field, after, top, bottom, own, sems):
    rows = pl.ds(pl.multiple_of(lax.axis_index("inst") * 16, 16), 16)
    copies = [
        pltpu.make_async_copy(field.at[b, plane], out.at[b], sems.at[k, b])
        for k, (plane, out) in enumerate(((field.shape[1] - 1, top), (0, bottom)))
        for b in range(field.shape[0])
    ]
    last = field.shape[1] - 1
    copies.append(
        pltpu.make_async_copy(field.at[:, 1:, rows, :], own.at[:, :last], sems.at[2, 0])
    )
    copies.append(
        pltpu.make_async_copy(field.at[:, :1, rows, :], own.at[:, last:], sems.at[2, 1])
    )
    for one in copies:
        one.start()
    for one in copies:
        one.wait()


def pack(field, planes):
    blocks, _, rows, lanes = field.shape
    size = sum(size for _, size in planes)
    return pl.pallas_call(
        functools.partial(pack_kernel, planes),
        out_shape=(shaped(blocks, size, rows // 4, lanes),) * 3,
        in_specs=[HBM],
        out_specs=(VMEM,) * 3,
        scratch_shapes=[pltpu.SemaphoreType.DMA((32,))],
        compiler_params=params(),
        cost_estimate=cost(),
    )(pltpu.with_memory_space_constraint(field, pltpu.HBM))


def turns(position, mode, orders, total):
    order = jnp.zeros(mode.shape, jnp.int32)
    count = orders.shape[0]
    for j in range(count):
        order = jnp.where((mode == 1 + j) | (mode == 1 + count + j), orders[j], order)
    phase = lax.rem(position * order, total).astype(jnp.float32) * (2.0 * math.pi / total)
    value = jnp.where(mode <= count, jnp.cos(phase), jnp.sin(phase))
    return jnp.where(mode <= 2 * count, value, 0.0)


def harmonics_kernel(total, orders, after, front, back, out):
    blocks, planes, _, lanes = front.shape
    mode = lax.broadcasted_iota(jnp.int32, (MODES, planes), 0)
    position = lax.broadcasted_iota(jnp.int32, (MODES, planes), 1) + lax.axis_index("mesh") * planes
    basis = turns(position, mode, orders, total) * jnp.where(mode == 0, 1.0 / total, 2.0 / total)
    rotor = lax.axis_index("row") == 0
    for b in range(blocks):
        edge = jnp.where(rotor, back[b, :, 7, :], front[b, :, 0, :])
        out[:, b * lanes : (b + 1) * lanes] = jnp.dot(
            basis, edge, precision=lax.Precision.HIGHEST, preferred_element_type=jnp.float32
        )


def mix_kernel(scalars, own, up, down, far, after, *outs):
    weight = [scalars[k] for k in range(INST)]
    cosine, sine = scalars[INST], scalars[INST + 1]
    at = jnp.where(lax.axis_index("mesh") == 0, 1, 0)

    def mixed(var):
        u = [r[s, var, at] for r in (own, up, far, down) for s in range(2)]
        sums = []
        for a in range(INST):
            total = weight[a % INST] * u[0]
            for b in range(1, INST):
                total = total + weight[(a - b) % INST] * u[b]
            sums.append(total)
        return sums

    half = INST // 2

    def put(var, values):
        for a, value in enumerate(values):
            outs[a // half][a % half, var] = value

    for var in (0, 1, 4, 5):
        put(var, mixed(var))
    v, w = mixed(2), mixed(3)
    put(2, [cosine * x - sine * y for x, y in zip(v, w)])
    put(3, [sine * x + cosine * y for x, y in zip(v, w)])


def source_kernel(rims, scalars, *refs):
    outs, refs = refs[-4:], refs[:-4]
    if rims:
        *ghost, nu = refs[-3:]
        refs = refs[:-3]
    size = len(refs) // 4
    own, up, down, far = (refs[k * size : (k + 1) * size] for k in range(4))
    ratio = scalars[0]
    c1, c2, c3 = (ratio * D1, ratio * D2, ratio * D3)
    out_own, out_up, out_down, out_far = outs
    order = (out_own, out_up, out_far, out_down)
    for var in range(up[0].shape[1]):
        for p in range(size):
            u = [own[p][s, var, 0] for s in range(2)]
            u += [r[p][s, var, 0] for r in (up, far, down) for s in range(2)]
            near = [u[(n - 1) % INST] - u[(n + 1) % INST] for n in range(INST)]
            second = [c2 * (u[(n - 2) % INST] - u[(n + 2) % INST]) for n in range(4)]
            for n in range(INST):
                s = c1 * near[n] - c3 * near[(n + 4) % INST]
                s = s + second[n] if n < 4 else s - second[n - 4]
                order[n // 2][n % 2, var, p] = s
    if not rims:
        return

    def add_ghost(p, factor):
        for var in range(up[0].shape[1]):
            for n in range(INST):
                at = (n % 2, var, p)
                order[n // 2][at] = order[n // 2][at] - factor * ghost[n // 4][n % 4, var]

    place = pl.ds(pl.multiple_of(lax.axis_index("inst") * 16, 16), 16)

    @pl.when(lax.axis_index("mesh") == 0)
    def _():
        add_ghost(size - 1, nu[0, place, :] + 0.5)

    @pl.when(lax.axis_index("mesh") == lax.axis_size("mesh") - 1)
    def _():
        add_ghost(size - 2, nu[nu.shape[0] - 1, place, :])


def stencil_kernel(nu, low, high, field, one, two):
    blocks, planes, rows, lanes = field.shape
    lane = lax.broadcasted_iota(jnp.int32, (rows, lanes), 1)
    row = lax.broadcasted_iota(jnp.int32, (rows, lanes), 0)
    for b in range(blocks):
        for p in range(planes):
            u = field[b, p]
            before = low[b] if p == 0 else field[b, p - 1]
            after = high[b] if p == planes - 1 else field[b, p + 1]
            left = jnp.where(lane == 0, 0.0, pltpu.roll(u, 1, 1))
            right = jnp.where(lane == lanes - 1, 0.0, pltpu.roll(u, lanes - 1, 1))
            above = jnp.where(row == 0, 0.0, pltpu.roll(u, 1, 0))
            below = jnp.where(row == rows - 1, 0.0, pltpu.roll(u, rows - 1, 0))
            lap = (before + after) + (above + below) + (left + right) - 6.0 * u
            at = (p - 1) % planes
            out, at = (one, at) if at < OUTER else (two, at - OUTER)
            out[b, at] = nu[p] * lap - (u - above) - 0.5 * (u - before)


def add_kernel(one, two, after, out):
    out[...] = one[...] + two[...]


def edge_kernel(total, orders, one, two, nu, *rest):
    out = rest[-1]
    planes, blocks, rows, lanes = out.shape
    mode = lax.broadcasted_iota(jnp.int32, (planes, MODES), 1)
    position = lax.broadcasted_iota(jnp.int32, (planes, MODES), 0) + lax.axis_index("mesh") * planes
    ghost = jnp.dot(
        turns(position, mode, orders, total),
        one[...] + two[...],
        precision=lax.Precision.HIGHEST,
        preferred_element_type=jnp.float32,
    )
    rotor = lax.axis_index("row") == 0
    hit = lax.broadcasted_iota(jnp.int32, (rows, lanes), 0) == jnp.where(rotor, rows - 1, 0)
    for p in range(planes):
        facing = jnp.where(rotor, nu[p, nu.shape[1] - 1 :, :], nu[p, :1, :] + 1.0)
        for b in range(blocks):
            value = facing * ghost[p : p + 1, b * lanes : (b + 1) * lanes]
            out[p, b] = jnp.where(hit, value, 0.0)


def final_kernel(start, chunk, near, inverse, edge, field, pre, *rest):
    new, residual, new_held, residual_held = rest[-6 - 2 * (not near) : -2 - 2 * (not near)]
    sems_in, sems = rest[-2:]
    count, planes, rows, lanes = field.shape
    size = pre.shape[1]
    base = (start + 1) % planes
    inst = lax.axis_index("inst")
    steps = (0, 1, 3, 2)
    arrivals = []
    if not near:
        held_in, pieces = rest[-4:-2]
    for b in range(0, count, chunk):
        if near:
            arrivals.append([])
            continue
        part = slice(b, b + chunk)
        pairs = [(pre.at[part], held_in.at[part])]
        pairs += [
            (rest[k].at[part], pieces.at[lax.rem(inst + step, 4), part])
            for k, step in enumerate(steps)
        ]
        arrivals.append(
            [
                pltpu.make_async_copy(x, y, sems_in.at[b // chunk, k])
                for k, (x, y) in enumerate(pairs)
            ]
        )
        for one in arrivals[-1]:
            one.start()
    tile = pl.ds(pl.multiple_of((1 - lax.axis_index("row")) * (rows - 8), 8), 8)
    runs = [(0, base, min(size, planes - base))]
    if base + size > planes:
        runs.append((planes - base, 0, base + size - planes))
    copies = []
    for j in range(0, count, 2):
        if j % chunk == 0:
            for one in arrivals[j // chunk]:
                one.wait()
        for p in range(size):
            plane = (base + p) % planes
            for b in (j, j + 1):
                for k, step in enumerate(steps):
                    if near:
                        at = pl.ds(pl.multiple_of(16 * lax.rem(inst + step, 4), 16), 16)
                        residual_held[b, p, at] = pre[b, p, at] - rest[k][b, p]
                    else:
                        at = pl.ds(16 * k, 16)
                        residual_held[b, p, at] = held_in[b, p, at] - pieces[k, b, p]
                residual_held[b, p, tile] = residual_held[b, p, tile] + edge[plane, b]
            high, low = split_bf16(
                jnp.concatenate([residual_held[j, p], residual_held[j + 1, p]], 1)
            )
            change = jnp.dot(
                inverse[...],
                jnp.concatenate([high, high, low], 0),
                preferred_element_type=jnp.float32,
            )
            new_held[j, p] = field[j, plane] + change[:, :lanes]
            new_held[j + 1, p] = field[j + 1, plane] + change[:, lanes:]
        if (j + 2) % chunk == 0:
            part = slice(j + 2 - chunk, j + 2)
            for held, out in ((residual_held, residual), (new_held, new)):
                for source, target, length in runs:
                    copies.append(
                        pltpu.make_async_copy(
                            held.at[part, source : source + length],
                            out.at[part, target : target + length],
                            sems.at[len(copies)],
                        )
                    )
                    copies[-1].start()
    for one in copies:
        one.wait()


def lag_weights(lag):
    delta = jnp.arange(INST).astype(jnp.float32) - lag
    total = 1.0 + jnp.cos(math.pi * delta)
    for k in range(1, INST // 2):
        total = total + 2.0 * jnp.cos(2.0 * math.pi * k / INST * delta)
    return total / INST


def local(state, viscosity, blade_counts, mode_orders):
    _, local_inst, variables, planes, rows, lanes = state.shape
    quarter = rows // 4
    blocks = local_inst * variables
    mesh_count = lax.axis_size("mesh")
    total = planes * mesh_count
    which = lax.axis_index("row")
    inst = lax.axis_index("inst")
    mesh_idx = lax.axis_index("mesh")
    counts = blade_counts.astype(jnp.float32)
    ratio = counts[1 - which] / counts[which]
    angle = 2.0 * math.pi / counts[which]
    field = state.reshape(blocks, planes, rows, lanes)
    nu = viscosity[0]
    first = mesh_idx == 0
    last = mesh_idx == mesh_count - 1

    def along(x, step):
        return lax.ppermute(x, "inst", [(j, (j + step) % 4) for j in range(4)])

    def in_hbm(*arrays):
        return [pltpu.with_memory_space_constraint(x, pltpu.HBM) for x in arrays]

    def exchange(up, down, far):
        from_down, from_up, from_far = along(up, 1), along(down, 3), along(far, 2)
        return from_up, from_down, from_far

    packed = pack(field, ((1, planes - 1), (0, 1)))
    gathered = exchange(*packed)

    top, bottom, own = pl.pallas_call(
        edges_kernel,
        out_shape=(shaped(blocks, rows, lanes),) * 2 + (shaped(blocks, planes, quarter, lanes),),
        in_specs=[HBM, VMEM],
        out_specs=(VMEM,) * 3,
        scratch_shapes=[pltpu.SemaphoreType.DMA((3, blocks))],
        compiler_params=params(),
        cost_estimate=cost(),
    )(pltpu.with_memory_space_constraint(field, pltpu.HBM), packed[0])
    low = lax.ppermute(top, "mesh", [(j, j + 1) for j in range(mesh_count - 1)])
    high = lax.ppermute(bottom, "mesh", [(j + 1, j) for j in range(mesh_count - 1)])

    split = (local_inst, variables)
    all_quarters = in_hbm(*(x.reshape(*split, planes, quarter, lanes) for x in (own, *gathered)))

    whole = shaped(*field.shape)
    at_once = 2
    slab = pl.BlockSpec((at_once, planes, rows, lanes), lambda b: (b, 0, 0, 0))
    plane = pl.BlockSpec((at_once, rows, lanes), lambda b: (b, 0, 0))
    pre_one, pre_two = pl.pallas_call(
        stencil_kernel,
        grid=(blocks // at_once,),
        out_shape=(
            pltpu.HBM((blocks, OUTER, rows, lanes), jnp.float32),
            pltpu.HBM((blocks, planes - OUTER, rows, lanes), jnp.float32),
        ),
        in_specs=[pl.BlockSpec((planes, rows, lanes), lambda b: (0, 0, 0)), plane, plane, slab],
        out_specs=(
            pl.BlockSpec((at_once, OUTER, rows, lanes), lambda b: (b, 0, 0, 0)),
            pl.BlockSpec((at_once, planes - OUTER, rows, lanes), lambda b: (b, 0, 0, 0)),
        ),
        compiler_params=params(),
        cost_estimate=cost(),
    )(nu, *in_hbm(low, high), field)

    harmonics = pl.pallas_call(
        functools.partial(harmonics_kernel, total),
        out_shape=shaped(MODES, blocks * lanes),
        grid=(1,),
        in_specs=[
            SMEM,
            VMEM,
            pl.BlockSpec((blocks, planes, 8, lanes), lambda b: (0, 0, 0, 0)),
            pl.BlockSpec((blocks, planes, 8, lanes), lambda b: (0, 0, rows // 8 - 1, 0)),
        ],
        out_specs=pl.BlockSpec((MODES, blocks * lanes), lambda b: (0, 0)),
        compiler_params=params(),
        cost_estimate=cost(),
    )(mode_orders, packed[0], field, field)

    def crossing(flip):
        return [
            (r * mesh_count + m, (1 - r) * mesh_count + (m ^ flip))
            for r in range(2)
            for m in range(mesh_count)
        ]

    def doubled(x, flip):
        return x + lax.ppermute(x, "mesh", [(m, m ^ flip) for m in range(mesh_count)])

    two_ways = [lax.ppermute(harmonics, ("row", "mesh"), crossing(flip)) for flip in (0, 1)]
    harmonics = two_ways[0] + two_ways[1]
    early = lax.ppermute(harmonics, "mesh", [(m, m ^ 2) for m in range(mesh_count)])

    def sources(start, size, rims, after=()):
        at_once = 3
        pieces_in = [
            pl.BlockSpec(
                (2, at_once, 1, quarter, lanes),
                functools.partial(lambda plane, b: (0, b, plane, 0, 0), start + p),
            )
            for _ in range(4)
            for p in range(size)
        ]
        rim_specs = [
            pl.BlockSpec((INST // 2, at_once, quarter, lanes), lambda b: (0, b, 0, 0)),
            pl.BlockSpec((INST // 2, at_once, quarter, lanes), lambda b: (0, b, 0, 0)),
            pl.BlockSpec((planes, rows, lanes), lambda b: (0, 0, 0)),
        ]
        def kernel(*refs):
            inputs, outputs = refs[: -4 - len(after)], refs[-4:]
            source_kernel(bool(rims), *inputs, *outputs)

        outs = pl.pallas_call(
            kernel,
            out_shape=(pltpu.HBM((*split, size, quarter, lanes), jnp.float32),) * 4,
            grid=(variables // at_once,),
            in_specs=[SMEM] + pieces_in + rim_specs[: len(rims)] + [ANY] * len(after),
            out_specs=(
                pl.BlockSpec((2, at_once, size, quarter, lanes), lambda b: (0, b, 0, 0, 0)),
            )
            * 4,
            compiler_params=params(),
            cost_estimate=cost(),
        )(ratio[None], *(x for x in all_quarters for _ in range(size)), *rims, *after)
        own, up, down, far = (x.reshape(blocks, size, quarter, lanes) for x in outs)
        return (own, *exchange(up, down, far))

    one_source = sources(0, OUTER, (), after=(*in_hbm(pre_one), early))

    weights = lag_weights(jnp.where(first, -ratio, ratio))
    turn = jnp.where(first, angle, -angle)
    ghost_shape = shaped(INST // 2, variables, quarter, lanes)

    outermost = pl.BlockSpec((2, variables, 2, quarter, lanes), lambda b: (0, 0, 3, 0, 0))
    ghost_out = pl.pallas_call(
        mix_kernel,
        out_shape=(ghost_shape,) * 2,
        grid=(1,),
        in_specs=[SMEM] + [outermost] * 4 + [ANY],
        out_specs=(pl.BlockSpec(ghost_shape.shape, lambda b: (0, 0, 0, 0)),) * 2,
        compiler_params=params(),
        cost_estimate=cost(),
    )(
        jnp.concatenate([weights, jnp.stack([jnp.cos(turn), jnp.sin(turn)])]),
        *all_quarters,
        *in_hbm(one_source[0]),
    )
    ghost = [
        lax.ppermute(part, "mesh", [(mesh_count - 1, 0), (0, mesh_count - 1)]) for part in ghost_out
    ]

    harmonics = pl.pallas_call(
        add_kernel,
        out_shape=harmonics,
        in_specs=[VMEM, VMEM, ANY],
        out_specs=VMEM,
        compiler_params=params(),
        cost_estimate=cost(),
    )(harmonics, early, ghost_out[0])
    harmonics = doubled(harmonics, 4)
    opposite = lax.ppermute(harmonics, "mesh", [(m, m ^ 8) for m in range(mesh_count)])
    two_source = sources(OUTER, planes - OUTER, (*ghost, nu), after=(opposite,))

    edge = pl.pallas_call(
        functools.partial(edge_kernel, total),
        out_shape=shaped(planes, blocks, 8, lanes),
        in_specs=[SMEM, VMEM, VMEM, VMEM] + [ANY] * 3,
        out_specs=VMEM,
        compiler_params=params(),
        cost_estimate=cost(),
    )(
        mode_orders,
        harmonics,
        opposite,
        nu,
        *one_source[1:],
    )

    inverse = jnp.asarray(inverse_parts(rows))
    kept = ()
    for start, size, group, pre in ((0, OUTER, one_source, pre_one), (OUTER, planes - OUTER, two_source, pre_two)):
        given = 4 + len(group)
        near = size < 4
        if near:
            group = [pltpu.with_memory_space_constraint(x, pltpu.VMEM) for x in group]
            given_in = (pre, *group)
        else:
            given_in = (*in_hbm(pre, group[0]), *group[1:])
        kept = pl.pallas_call(
            functools.partial(final_kernel, start, 4 if near else 2, near),
            out_shape=(pltpu.HBM(field.shape, jnp.float32),) * 2,
            in_specs=[VMEM] * 3
            + ([VMEM] * 5 if near else [HBM] * 2 + [ANY] * 3)
            + [HBM] * len(kept),
            out_specs=(HBM,) * 2,
            scratch_shapes=[pltpu.VMEM((blocks, size, rows, lanes), jnp.float32)] * (2 + (not near))
            + [pltpu.VMEM((4, blocks, size, quarter, lanes), jnp.float32)] * (not near)
            + [pltpu.SemaphoreType.DMA((blocks, 5)), pltpu.SemaphoreType.DMA((4 * blocks,))],
            input_output_aliases={given: 0, given + 1: 1} if kept else {},
            compiler_params=params(),
            cost_estimate=cost(),
        )(inverse, edge, field, *given_in, *kept)
    new, residual = kept
    return (new.reshape(state.shape), residual.reshape(state.shape))


def solution(mesh):
    spread = P("row", "inst", None, "mesh", None, None)
    return jax.shard_map(
        local,
        mesh=mesh,
        in_specs=(spread, P("row", "mesh", None, None), P(), P()),
        out_specs=(spread, spread),
        check_vma=False,
    )
```

profile of v0, /device:TPU:97, one launch (start us, length us, event | category | flops | bytes accessed | tf_op | source)
XLA Modules:
  0.0 89.0 jit_solution(9739779839727823778)
XLA Ops:
  0.7 3.6 %shard_map.68 = (f32[12,8,16,128]{3,2,1,0:T(8,128)}, f32[12,8,16,128]{3,2,1,0:T(8,128)}, f32[12,8,16,128]{3,2,1,0:T(8,128)}) custom-call(f32[12,8,64,128]{3,2,1,0:T(8,128)} %bitcast.20), custom_call_target="tpu_custom_call" | custom-call | flops 1 | bytes 1 | tf_op jit(solution)/shard_map/pallas_call | solution.py:103
  4.2 2.5 %collective-permute-start.3 = (f32[12,8,16,128]{3,2,1,0:T(8,128)}, f32[12,8,16,128]{3,2,1,0:T(8,128)}, u32[]{:S(2)}, u32[]{:S(2)}) collective-permute-start(f32[12,8,16,128]{3,2,1,0:T(8,128)} %get-tuple-element.26), channel_id=1, source_target_pairs={{0,48},{16,0},{32,16},{48,32},{1,49},{17,1},{33,17},{49,33},{2,50}... | collective-permute-start | bytes 2359304 | tf_op jit(solution)/shard_map/ppermute | solution.py:350
  7.9 1.6 %shard_map.69 = f32[24,1536]{1,0:T(8,128)S(1)} custom-call(s32[8]{0:T(128)S(1)} %copy-done.7, f32[12,8,16,128]{3,2,1,0:T(8,128)} %get-tuple-element.24.after, f32[12,8,64,128]{3,2,1,0:T(8,128)S(1)} %bitcast.22, f32[12,8,64,128]{3,2,1,0:T(8,128)S(1)} %bitcast.23), custom_call_target="tpu_custom_call" | custom-call | flops 1 | bytes 1 | tf_op jit(solution)/shard_map/pallas_call | solution.py:397
  9.6 4.4 %collective-permute-start.1 = (f32[24,1536]{1,0:T(8,128)S(1)}, f32[24,1536]{1,0:T(8,128)S(1)}, u32[]{:S(2)}, u32[]{:S(2)}) collective-permute-start(f32[24,1536]{1,0:T(8,128)S(1)} %shard_map.69), channel_id=1, source_target_pairs={{0,65},{1,64},{2,67},{3,66},{4,69},{5,68},{6,71},{7,70},{8,73},{9,... | collective-permute-start | bytes 442376 | tf_op jit(solution)/shard_map/ppermute | solution.py:422
  14.0 3.7 %shard_map.70 = (f32[12,64,128]{2,1,0:T(8,128)S(1)}, f32[12,64,128]{2,1,0:T(8,128)}, f32[12,8,16,128]{3,2,1,0:T(8,128)S(1)}) custom-call(f32[12,8,64,128]{3,2,1,0:T(8,128)} %bitcast.21, f32[12,8,16,128]{3,2,1,0:T(8,128)} %get-tuple-element.24.after), custom_call_target="tpu_custom_call" | custom-call | flops 1 | bytes 1 | tf_op jit(solution)/shard_map/pallas_call | solution.py:362
  18.7 1.9 %collective-permute-start.6 = (f32[12,64,128]{2,1,0:T(8,128)S(1)}, f32[12,64,128]{2,1,0:T(8,128)S(1)}, u32[]{:S(2)}, u32[]{:S(2)}) collective-permute-start(f32[12,64,128]{2,1,0:T(8,128)S(1)} %get-tuple-element.28), channel_id=1, source_target_pairs={{0,1},{1,2},{2,3},{3,4},{4,5},{5,6},{6,7},{7,8},{8,9},{9,10},{10,1... | collective-permute-start | bytes 1179656 | tf_op jit(solution)/shard_map/ppermute | solution.py:371
  21.5 2.4 %collective-permute-start.7 = (f32[12,64,128]{2,1,0:T(8,128)}, f32[12,64,128]{2,1,0:T(8,128)}, u32[]{:S(2)}, u32[]{:S(2)}) collective-permute-start(f32[12,64,128]{2,1,0:T(8,128)} %get-tuple-element.29), channel_id=1, source_target_pairs={{1,0},{2,1},{3,2},{4,3},{5,4},{6,5},{7,6},{8,7},{9,8},{10,9},{11,1... | collective-permute-start | bytes 1179656 | tf_op jit(solution)/shard_map/ppermute | solution.py:372
  23.9 1.4 %collective-permute-done.6.low = f32[12,64,128]{2,1,0:T(8,128)S(1)} collective-permute-done((f32[12,64,128]{2,1,0:T(8,128)S(1)}, f32[12,64,128]{2,1,0:T(8,128)S(1)}, u32[]{:S(2)}, u32[]{:S(2)}) %collective-permute-start.6) | collective-permute-done | bytes 393248 | tf_op jit(solution)/shard_map/ppermute | solution.py:371
  26.1 1.7 %collective-permute-start.2 = (f32[24,1536]{1,0:T(8,128)S(1)}, f32[24,1536]{1,0:T(8,128)}, u32[]{:S(2)}, u32[]{:S(2)}) collective-permute-start(f32[24,1536]{1,0:T(8,128)S(1)} %add.26.one), channel_id=1, source_target_pairs={{0,2},{1,3},{2,0},{3,1},{4,6},{5,7},{6,4},{7,5},{8,10},{9,11},{10,... | collective-permute-start | bytes 442376 | tf_op jit(solution)/shard_map/ppermute | solution.py:424
  29.0 1.4 %fusion = (f32[1]{0:T(128)}, f32[1]{0:T(128)}) fusion(f32[2]{0:T(128)} %convert_element_type.7, s32[]{:T(128)S(6)} %select_n.14, s32[]{:T(128)S(6)} %select_n.15), kind=kLoop, calls=%fused_computation.2 | loop fusion | bytes 24 | tf_op jit(solution)/shard_map/dynamic_slice | solution.py:342
  33.0 5.6 %shard_map.71 = (f32[12,6,64,128]{3,2,1,0:T(8,128)}, f32[12,2,64,128]{3,2,1,0:T(8,128)}) custom-call(f32[8,64,128]{2,1,0:T(8,128)S(1)} %bitcast.36, f32[12,64,128]{2,1,0:T(8,128)} %copy-done.9, f32[12,64,128]{2,1,0:T(8,128)} %collective-permute-done.7.high, f32[12,8,64,128]{3,2,1,0:T(8,128)S(1)} %bitcast.24), custom_call_target="tpu_custom_call" | custom-call | flops 1 | bytes 1 | tf_op jit(solution)/shard_map/pallas_call | solution.py:381
  38.6 6.3 %collective-permute-done.4 = f32[12,8,16,128]{3,2,1,0:T(8,128)} collective-permute-done((f32[12,8,16,128]{3,2,1,0:T(8,128)}, f32[12,8,16,128]{3,2,1,0:T(8,128)}, u32[]{:S(2)}, u32[]{:S(2)}) %collective-permute-start.4) | collective-permute-done | bytes 786464 | tf_op jit(solution)/shard_map/ppermute | solution.py:350
  44.9 3.0 %shard_map.72 = (f32[2,6,6,16,128]{4,3,2,1,0:T(8,128)}, f32[2,6,6,16,128]{4,3,2,1,0:T(8,128)}, f32[2,6,6,16,128]{4,3,2,1,0:T(8,128)}, f32[2,6,6,16,128]{4,3,2,1,0:T(8,128)}) custom-call(f32[1]{0:T(128)} %div.15.refs_0_, f32[2,6,8,16,128]{4,3,2,1,0:T(8,128)} %bitcast.27, f32[2,6,8,16,128]{4,3,2,1,0:T(8,128)} %bitcast.28, f32[2,6,8,16,128]{4,3,2,1,0:T(8,128)} %bitcast.29, ...), custom_call_target="tpu_custom_call" | custom-call | flops 1 | bytes 1 | tf_op jit(solution)/shard_map/pallas_call | solution.py:445
  48.9 1.5 %collective-permute-start.11 = (f32[12,6,16,128]{3,2,1,0:T(8,128)}, f32[12,6,16,128]{3,2,1,0:T(8,128)S(1)}, u32[]{:S(2)}, u32[]{:S(2)}) collective-permute-start(f32[12,6,16,128]{3,2,1,0:T(8,128)} %bitcast.45), channel_id=1, source_target_pairs={{0,16},{16,32},{32,48},{48,0},{1,17},{17,33},{33,49},{49,1},{2,18}... | collective-permute-start | bytes 1769480 | tf_op jit(solution)/shard_map/ppermute | solution.py:350
  51.0 1.4 %shard_map.73 = (f32[4,6,16,128]{3,2,1,0:T(8,128)S(1)}, f32[4,6,16,128]{3,2,1,0:T(8,128)S(1)}) custom-call(f32[10]{0:T(128)S(1)} %pad_maximum_fusion.scalars, f32[2,6,8,16,128]{4,3,2,1,0:T(8,128)} %bitcast.33, f32[2,6,8,16,128]{4,3,2,1,0:T(8,128)} %bitcast.6.refs_7_.refs_8_.refs_9_.refs_10_.refs_11_.refs_12_.up.refs_3_.refs_4_, ...), custom_call_target="tpu_custom_call" | custom-call | flops 1 | bytes 1 | tf_op jit(solution)/shard_map/pallas_call | solution.py:467
  54.4 4.6 %collective-permute-done.8 = f32[24,1536]{1,0:T(8,128)S(1)} collective-permute-done((f32[24,1536]{1,0:T(8,128)S(1)}, f32[24,1536]{1,0:T(8,128)S(1)}, u32[]{:S(2)}, u32[]{:S(2)}) %collective-permute-start.8) | collective-permute-done | bytes 147488 | tf_op jit(solution)/shard_map/ppermute | solution.py:420
  59.7 5.8 %collective-permute-start.9 = (f32[24,1536]{1,0:T(8,128)S(1)}, f32[24,1536]{1,0:T(8,128)S(1)}, u32[]{:S(2)}, u32[]{:S(2)}) collective-permute-start(f32[24,1536]{1,0:T(8,128)S(1)} %add.33.one), channel_id=1, source_target_pairs={{0,8},{1,9},{2,10},{3,11},{4,12},{5,13},{6,14},{7,15},{8,0},{9,1},... | collective-permute-start | bytes 442376 | tf_op jit(solution)/shard_map/ppermute | solution.py:493
  65.6 4.7 %collective-permute-done.9.two.refs_12_ = f32[24,1536]{1,0:T(8,128)S(1)} collective-permute-done((f32[24,1536]{1,0:T(8,128)S(1)}, f32[24,1536]{1,0:T(8,128)S(1)}, u32[]{:S(2)}, u32[]{:S(2)}) %collective-permute-start.9) | collective-permute-done | bytes 147488 | tf_op jit(solution)/shard_map/ppermute | solution.py:493
  70.3 2.1 %shard_map.76 = (f32[2,6,2,16,128]{4,3,2,1,0:T(8,128)}, f32[2,6,2,16,128]{4,3,2,1,0:T(8,128)}, f32[2,6,2,16,128]{4,3,2,1,0:T(8,128)}, f32[2,6,2,16,128]{4,3,2,1,0:T(8,128)}) custom-call(f32[1]{0:T(128)} %div.15.refs_0_, f32[2,6,8,16,128]{4,3,2,1,0:T(8,128)} %bitcast.34, f32[2,6,8,16,128]{4,3,2,1,0:T(8,128)} %bitcast.35, ...), custom_call_target="tpu_custom_call" | custom-call | flops 1 | bytes 1 | tf_op jit(solution)/shard_map/pallas_call | solution.py:445
  72.3 2.0 %collective-permute-start.15 = (f32[12,2,16,128]{3,2,1,0:T(8,128)}, f32[12,2,16,128]{3,2,1,0:T(8,128)S(1)}, u32[]{:S(2)}, u32[]{:S(2)}) collective-permute-start(f32[12,2,16,128]{3,2,1,0:T(8,128)} %bitcast.49), channel_id=1, source_target_pairs={{0,48},{16,0},{32,16},{48,32},{1,49},{17,1},{33,17},{49,33},{2,50}... | collective-permute-start | bytes 589832 | tf_op jit(solution)/shard_map/ppermute | solution.py:350
  74.4 1.9 %collective-permute-start.17 = (f32[12,2,16,128]{3,2,1,0:T(8,128)}, f32[12,2,16,128]{3,2,1,0:T(8,128)S(1)}, u32[]{:S(2)}, u32[]{:S(2)}) collective-permute-start(f32[12,2,16,128]{3,2,1,0:T(8,128)} %bitcast.47), channel_id=1, source_target_pairs={{0,32},{16,48},{32,0},{48,16},{1,33},{17,49},{33,1},{49,17},{2,34}... | collective-permute-start | bytes 589832 | tf_op jit(solution)/shard_map/ppermute | solution.py:350
  77.3 5.0 %shard_map.77 = (f32[12,8,64,128]{3,2,1,0:T(8,128)}, f32[12,8,64,128]{3,2,1,0:T(8,128)}) custom-call(bf16[64,192]{1,0:T(8,128)(2,1)S(1)} %copy-done.6, f32[8,12,8,128]{3,2,1,0:T(8,128)S(1)} %shard_map.75.edge, f32[12,8,64,128]{3,2,1,0:T(8,128)S(1)} %bitcast.25, f32[12,6,64,128]{3,2,1,0:T(8,128)} %get-tuple-element.30.refs_25_.pre, ...), custom_call_target="tpu_custom_call" | custom-call | flops 1 | bytes 1 | tf_op jit(solution)/shard_map/pallas_call | solution.py:521
  82.4 4.3 %collective-permute-done.16.rest_2_ = f32[12,2,16,128]{3,2,1,0:T(8,128)S(1)} collective-permute-done((f32[12,2,16,128]{3,2,1,0:T(8,128)}, f32[12,2,16,128]{3,2,1,0:T(8,128)S(1)}, u32[]{:S(2)}, u32[]{:S(2)}) %collective-permute-start.16) | collective-permute-done | bytes 196640 | tf_op jit(solution)/shard_map/ppermute | solution.py:350
  86.7 2.3 %shard_map.78 = (f32[12,8,64,128]{3,2,1,0:T(8,128)}, f32[12,8,64,128]{3,2,1,0:T(8,128)}) custom-call(bf16[64,192]{1,0:T(8,128)(2,1)S(1)} %copy-done.6, f32[8,12,8,128]{3,2,1,0:T(8,128)S(1)} %shard_map.75.edge, f32[12,8,64,128]{3,2,1,0:T(8,128)S(1)} %bitcast.26, f32[12,2,64,128]{3,2,1,0:T(8,128)S(1)} %copy-done.4, ...), custom_call_target="tpu_custom_call", output_to_operand_aliasing={{0}: (8, {}), {1}: (9, {})} | custom-call | flops 1 | bytes 1 | tf_op jit(solution)/shard_map/pallas_call | solution.py:521
  (49 shorter events, 10.7 us)
Async XLA Ops:
  4.2 34.4 %collective-permute-start.3 = (f32[12,8,16,128]{3,2,1,0:T(8,128)}, f32[12,8,16,128]{3,2,1,0:T(8,128)}, u32[]{:S(2)}, u32[]{:S(2)}) collective-permute-start(f32[12,8,16,128]{3,2,1,0:T(8,128)} %get-tuple-element.26), channel_id=1, source_target_pairs={{0,48},{16,0},{32,16},{48,32},{1,49},{17,1},{33,17},{49,33},{2,50}... | collective-permute-start | bytes 2359304 | tf_op jit(solution)/shard_map/ppermute | solution.py:350
  6.8 31.8 %collective-permute-start.5 = (f32[12,8,16,128]{3,2,1,0:T(8,128)}, f32[12,8,16,128]{3,2,1,0:T(8,128)}, u32[]{:S(2)}, u32[]{:S(2)}) collective-permute-start(f32[12,8,16,128]{3,2,1,0:T(8,128)} %get-tuple-element.27), channel_id=1, source_target_pairs={{0,32},{16,48},{32,0},{48,16},{1,33},{17,49},{33,1},{49,17},{2,34}... | collective-permute-start | bytes 2359304 | tf_op jit(solution)/shard_map/ppermute | solution.py:350
  7.3 37.6 %collective-permute-start.4 = (f32[12,8,16,128]{3,2,1,0:T(8,128)}, f32[12,8,16,128]{3,2,1,0:T(8,128)}, u32[]{:S(2)}, u32[]{:S(2)}) collective-permute-start(f32[12,8,16,128]{3,2,1,0:T(8,128)} %get-tuple-element.24.after), channel_id=1, source_target_pairs={{0,16},{16,32},{32,48},{48,0},{1,17},{17,33},{33,49},{49,1},{2,18}... | collective-permute-start | bytes 2359304 | tf_op jit(solution)/shard_map/ppermute | solution.py:350
  9.5 23.4 %copy-start.1 = (f32[1,2,6,8,64,128]{5,4,3,2,1,0:T(8,128)S(1)}, f32[1,2,6,8,64,128]{5,4,3,2,1,0:T(8,128)}, u32[]{:S(2)}) copy-start(f32[1,2,6,8,64,128]{5,4,3,2,1,0:T(8,128)} %param.5) | copy-start | bytes 9437188
  9.6 23.4 %copy-start.3 = (f32[1,8,64,128]{3,2,1,0:T(8,128)S(1)}, f32[1,8,64,128]{3,2,1,0:T(8,128)}, u32[]{:S(2)}) copy-start(f32[1,8,64,128]{3,2,1,0:T(8,128)} %param.6) | copy-start | bytes 786436
  9.6 9.1 %collective-permute-start.1 = (f32[24,1536]{1,0:T(8,128)S(1)}, f32[24,1536]{1,0:T(8,128)S(1)}, u32[]{:S(2)}, u32[]{:S(2)}) collective-permute-start(f32[24,1536]{1,0:T(8,128)S(1)} %shard_map.69), channel_id=1, source_target_pairs={{0,65},{1,64},{2,67},{3,66},{4,69},{5,68},{6,71},{7,70},{8,73},{9,... | collective-permute-start | bytes 442376 | tf_op jit(solution)/shard_map/ppermute | solution.py:422
  13.9 7.5 %collective-permute-start = (f32[24,1536]{1,0:T(8,128)S(1)}, f32[24,1536]{1,0:T(8,128)S(1)}, u32[]{:S(2)}, u32[]{:S(2)}) collective-permute-start(f32[24,1536]{1,0:T(8,128)S(1)} %shard_map.69), channel_id=1, source_target_pairs={{0,64},{1,65},{2,66},{3,67},{4,68},{5,69},{6,70},{7,71},{8,72},{9,... | collective-permute-start | bytes 442376 | tf_op jit(solution)/shard_map/ppermute | solution.py:422
  18.7 6.6 %collective-permute-start.6 = (f32[12,64,128]{2,1,0:T(8,128)S(1)}, f32[12,64,128]{2,1,0:T(8,128)S(1)}, u32[]{:S(2)}, u32[]{:S(2)}) collective-permute-start(f32[12,64,128]{2,1,0:T(8,128)S(1)} %get-tuple-element.28), channel_id=1, source_target_pairs={{0,1},{1,2},{2,3},{3,4},{4,5},{5,6},{6,7},{7,8},{8,9},{9,10},{10,1... | collective-permute-start | bytes 1179656 | tf_op jit(solution)/shard_map/ppermute | solution.py:371
  21.5 11.5 %collective-permute-start.7 = (f32[12,64,128]{2,1,0:T(8,128)}, f32[12,64,128]{2,1,0:T(8,128)}, u32[]{:S(2)}, u32[]{:S(2)}) collective-permute-start(f32[12,64,128]{2,1,0:T(8,128)} %get-tuple-element.29), channel_id=1, source_target_pairs={{1,0},{2,1},{3,2},{4,3},{5,4},{6,5},{7,6},{8,7},{9,8},{10,9},{11,1... | collective-permute-start | bytes 1179656 | tf_op jit(solution)/shard_map/ppermute | solution.py:372
  26.1 12.5 %collective-permute-start.2 = (f32[24,1536]{1,0:T(8,128)S(1)}, f32[24,1536]{1,0:T(8,128)}, u32[]{:S(2)}, u32[]{:S(2)}) collective-permute-start(f32[24,1536]{1,0:T(8,128)S(1)} %add.26.one), channel_id=1, source_target_pairs={{0,2},{1,3},{2,0},{3,1},{4,6},{5,7},{6,4},{7,5},{8,10},{9,11},{10,... | collective-permute-start | bytes 442376 | tf_op jit(solution)/shard_map/ppermute | solution.py:424
  47.9 26.4 %collective-permute-start.10 = (f32[12,6,16,128]{3,2,1,0:T(8,128)}, f32[12,6,16,128]{3,2,1,0:T(8,128)}, u32[]{:S(2)}, u32[]{:S(2)}) collective-permute-start(f32[12,6,16,128]{3,2,1,0:T(8,128)} %bitcast.46), channel_id=1, source_target_pairs={{0,48},{16,0},{32,16},{48,32},{1,49},{17,1},{33,17},{49,33},{2,50}... | collective-permute-start | bytes 1769480 | tf_op jit(solution)/shard_map/ppermute | solution.py:350
  48.9 27.4 %collective-permute-start.11 = (f32[12,6,16,128]{3,2,1,0:T(8,128)}, f32[12,6,16,128]{3,2,1,0:T(8,128)S(1)}, u32[]{:S(2)}, u32[]{:S(2)}) collective-permute-start(f32[12,6,16,128]{3,2,1,0:T(8,128)} %bitcast.45), channel_id=1, source_target_pairs={{0,16},{16,32},{32,48},{48,0},{1,17},{17,33},{33,49},{49,1},{2,18}... | collective-permute-start | bytes 1769480 | tf_op jit(solution)/shard_map/ppermute | solution.py:350
  50.4 26.0 %collective-permute-start.12 = (f32[12,6,16,128]{3,2,1,0:T(8,128)}, f32[12,6,16,128]{3,2,1,0:T(8,128)S(1)}, u32[]{:S(2)}, u32[]{:S(2)}) collective-permute-start(f32[12,6,16,128]{3,2,1,0:T(8,128)} %bitcast.44), channel_id=1, source_target_pairs={{0,32},{16,48},{32,0},{48,16},{1,33},{17,49},{33,1},{49,17},{2,34}... | collective-permute-start | bytes 1769480 | tf_op jit(solution)/shard_map/ppermute | solution.py:350
  53.4 5.6 %collective-permute-start.8 = (f32[24,1536]{1,0:T(8,128)S(1)}, f32[24,1536]{1,0:T(8,128)S(1)}, u32[]{:S(2)}, u32[]{:S(2)}) collective-permute-start(f32[24,1536]{1,0:T(8,128)S(1)} %shard_map.74), channel_id=1, source_target_pairs={{0,4},{1,5},{2,6},{3,7},{4,0},{5,1},{6,2},{7,3},{8,12},{9,13},{10,... | collective-permute-start | bytes 442376 | tf_op jit(solution)/shard_map/ppermute | solution.py:420
  53.8 5.9 %collective-permute-start.14 = (f32[4,6,16,128]{3,2,1,0:T(8,128)S(1)}, f32[4,6,16,128]{3,2,1,0:T(8,128)S(1)}, u32[]{:S(2)}, u32[]{:S(2)}) collective-permute-start(f32[4,6,16,128]{3,2,1,0:T(8,128)S(1)} %get-tuple-element.37), channel_id=1, source_target_pairs={{15,0},{0,15},{31,16},{16,31},{47,32},{32,47},{63,48},{48,63},{79,... | collective-permute-start | bytes 589832 | tf_op jit(solution)/shard_map/ppermute | solution.py:481
  59.0 6.6 %collective-permute-start.13 = (f32[4,6,16,128]{3,2,1,0:T(8,128)S(1)}, f32[4,6,16,128]{3,2,1,0:T(8,128)S(1)}, u32[]{:S(2)}, u32[]{:S(2)}) collective-permute-start(f32[4,6,16,128]{3,2,1,0:T(8,128)S(1)} %get-tuple-element.32.after), channel_id=1, source_target_pairs={{15,0},{0,15},{31,16},{16,31},{47,32},{32,47},{63,48},{48,63},{79,... | collective-permute-start | bytes 589832 | tf_op jit(solution)/shard_map/ppermute | solution.py:481
  59.7 16.8 %copy-start.8 = (s32[8]{0:T(128)S(1)}, s32[8]{0:T(128)}, u32[]{:S(2)}) copy-start(s32[8]{0:T(128)} %orders.3) | copy-start | bytes 100
  59.7 17.6 %copy-start.6 = (bf16[64,192]{1,0:T(8,128)(2,1)S(1)}, bf16[64,192]{1,0:T(8,128)(2,1)}, u32[]{:S(2)}) copy-start(bf16[64,192]{1,0:T(8,128)(2,1)} %constant.38.clone.inverse) | copy-start | bytes 73732
  59.7 10.6 %collective-permute-start.9 = (f32[24,1536]{1,0:T(8,128)S(1)}, f32[24,1536]{1,0:T(8,128)S(1)}, u32[]{:S(2)}, u32[]{:S(2)}) collective-permute-start(f32[24,1536]{1,0:T(8,128)S(1)} %add.33.one), channel_id=1, source_target_pairs={{0,8},{1,9},{2,10},{3,11},{4,12},{5,13},{6,14},{7,15},{8,0},{9,1},... | collective-permute-start | bytes 442376 | tf_op jit(solution)/shard_map/ppermute | solution.py:493
  72.3 10.1 %collective-permute-start.15 = (f32[12,2,16,128]{3,2,1,0:T(8,128)}, f32[12,2,16,128]{3,2,1,0:T(8,128)S(1)}, u32[]{:S(2)}, u32[]{:S(2)}) collective-permute-start(f32[12,2,16,128]{3,2,1,0:T(8,128)} %bitcast.49), channel_id=1, source_target_pairs={{0,48},{16,0},{32,16},{48,32},{1,49},{17,1},{33,17},{49,33},{2,50}... | collective-permute-start | bytes 589832 | tf_op jit(solution)/shard_map/ppermute | solution.py:350
  74.4 12.3 %collective-permute-start.16 = (f32[12,2,16,128]{3,2,1,0:T(8,128)}, f32[12,2,16,128]{3,2,1,0:T(8,128)S(1)}, u32[]{:S(2)}, u32[]{:S(2)}) collective-permute-start(f32[12,2,16,128]{3,2,1,0:T(8,128)} %bitcast.48), channel_id=1, source_target_pairs={{0,16},{16,32},{32,48},{48,0},{1,17},{17,33},{33,49},{49,1},{2,18}... | collective-permute-start | bytes 589832 | tf_op jit(solution)/shard_map/ppermute | solution.py:350
  74.4 12.3 %collective-permute-start.17 = (f32[12,2,16,128]{3,2,1,0:T(8,128)}, f32[12,2,16,128]{3,2,1,0:T(8,128)S(1)}, u32[]{:S(2)}, u32[]{:S(2)}) collective-permute-start(f32[12,2,16,128]{3,2,1,0:T(8,128)} %bitcast.47), channel_id=1, source_target_pairs={{0,32},{16,48},{32,0},{48,16},{1,33},{17,49},{33,1},{49,17},{2,34}... | collective-permute-start | bytes 589832 | tf_op jit(solution)/shard_map/ppermute | solution.py:350
  77.3 9.3 %copy-start.4 = (f32[12,2,64,128]{3,2,1,0:T(8,128)S(1)}, f32[12,2,64,128]{3,2,1,0:T(8,128)}, u32[]{:S(2)}) copy-start(f32[12,2,64,128]{3,2,1,0:T(8,128)} %get-tuple-element.36.pre) | copy-start | bytes 2359300
  77.3 9.3 %copy-start.5 = (f32[2,6,2,16,128]{4,3,2,1,0:T(8,128)S(1)}, f32[2,6,2,16,128]{4,3,2,1,0:T(8,128)}, u32[]{:S(2)}) copy-start(f32[2,6,2,16,128]{4,3,2,1,0:T(8,128)} %get-tuple-element.38) | copy-start | bytes 589828
  (4 other events, 16.2 us)
where the time goes:
time: 89.9 us; the launch traced here: 89 us
  Pallas kernels  30.1 us (33%)
  starting transfers between devices  27.7 us (31%)
  waiting for transfers between devices  23.7 us (26%)
  local copies, waits for them, and re-layouts  3.1 us (3%)
  between operations  3.02 us (3%)
  other arithmetic  1.41 us (2%)
    ppermute x9, waiting for transfers between devices, along(): return lax.ppermute(x, 'inst', [(j, (j + step) % 4) for j in range(4)])  10.7 us
    ppermute x9, starting transfers between devices, along(): return lax.ppermute(x, 'inst', [(j, (j + step) % 4) for j in range(4)])  9.77 us
    pallas_call x2, Pallas kernels, local(): pl.pallas_call(functools.partial(final_kernel, start, 4 if near else 2, n...  7.36 us
    ppermute x1, starting transfers between devices, local(): lax.ppermute(harmonics, 'mesh', [(m, m ^ 8) for m in range(mesh_count)])  5.83 us
    pallas_call x1, Pallas kernels, local(): pl.pallas_call(stencil_kernel, grid=(blocks // at_once,), out_shape=(pltp...  5.57 us
    pallas_call x2, Pallas kernels, sources(): pl.pallas_call(kernel, out_shape=(pltpu.HBM((*split, size, quarter, lanes...  5.07 us
    ppermute x1, waiting for transfers between devices, local(): lax.ppermute(harmonics, 'mesh', [(m, m ^ 8) for m in range(mesh_count)])  4.72 us
    ppermute x1, waiting for transfers between devices, doubled(): lax.ppermute(x, 'mesh', [(m, m ^ flip) for m in range(mesh_count)])  4.56 us
  transfers between devices with their start and end apart: 18, of which 9 were waited for; matrix products, arithmetic and copies ran while one was open for 3% of the time, Pallas kernels for 24%

commit v1 on v0

--- a/solution.py
+++ b/solution.py
@@ -138,9 +138,11 @@
     weight = [scalars[k] for k in range(INST)]
     cosine, sine = scalars[INST], scalars[INST + 1]
     at = jnp.where(lax.axis_index("mesh") == 0, 1, 0)
+    first = up.shape[2] - 2
 
     def mixed(var):
-        u = [r[s, var, at] for r in (own, up, far, down) for s in range(2)]
+        u = [own[s, var, at] for s in range(2)]
+        u += [r[s, var, first + at] for r in (up, far, down) for s in range(2)]
         sums = []
         for a in range(INST):
             total = weight[a % INST] * u[0]
@@ -162,21 +164,22 @@
     put(3, [sine * x + cosine * y for x, y in zip(v, w)])
 
 
-def source_kernel(rims, scalars, *refs):
+def source_kernel(rims, start, scalars, *refs):
     outs, refs = refs[-4:], refs[:-4]
     if rims:
         *ghost, nu = refs[-3:]
         refs = refs[:-3]
-    size = len(refs) // 4
-    own, up, down, far = (refs[k * size : (k + 1) * size] for k in range(4))
+    own, up, down, far = refs
+    at_once, size = outs[0].shape[1:3]
+    block = pl.program_id(0) * at_once
     ratio = scalars[0]
     c1, c2, c3 = (ratio * D1, ratio * D2, ratio * D3)
     out_own, out_up, out_down, out_far = outs
     order = (out_own, out_up, out_far, out_down)
-    for var in range(up[0].shape[1]):
+    for var in range(at_once):
         for p in range(size):
-            u = [own[p][s, var, 0] for s in range(2)]
-            u += [r[p][s, var, 0] for r in (up, far, down) for s in range(2)]
+            u = [own[s, var, start + p] for s in range(2)]
+            u += [r[s, block + var, start + p] for r in (up, far, down) for s in range(2)]
             near = [u[(n - 1) % INST] - u[(n + 1) % INST] for n in range(INST)]
             second = [c2 * (u[(n - 2) % INST] - u[(n + 2) % INST]) for n in range(4)]
             for n in range(INST):
@@ -187,10 +190,10 @@
         return
 
     def add_ghost(p, factor):
-        for var in range(up[0].shape[1]):
+        for var in range(at_once):
             for n in range(INST):
                 at = (n % 2, var, p)
-                order[n // 2][at] = order[n // 2][at] - factor * ghost[n // 4][n % 4, var]
+                order[n // 2][at] = order[n // 2][at] - factor * ghost[n // 4][n % 4, block + var]
 
     place = pl.ds(pl.multiple_of(lax.axis_index("inst") * 16, 16), 16)
 
@@ -352,6 +355,9 @@
     def in_hbm(*arrays):
         return [pltpu.with_memory_space_constraint(x, pltpu.HBM) for x in arrays]
 
+    def in_vmem(*arrays):
+        return [pltpu.with_memory_space_constraint(x, pltpu.VMEM) for x in arrays]
+
     def exchange(up, down, far):
         from_down, from_up, from_far = along(up, 1), along(down, 3), along(far, 2)
         return from_up, from_down, from_far
@@ -372,7 +378,8 @@
     high = lax.ppermute(bottom, "mesh", [(j + 1, j) for j in range(mesh_count - 1)])
 
     split = (local_inst, variables)
-    all_quarters = in_hbm(*(x.reshape(*split, planes, quarter, lanes) for x in (own, *gathered)))
+    own, *theirs = (x.reshape(*split, planes, quarter, lanes) for x in (own, *gathered))
+    all_quarters = (*in_hbm(own), *in_vmem(*theirs))
 
     whole = shaped(*field.shape)
     at_once = 2
@@ -424,36 +431,29 @@
     early = lax.ppermute(harmonics, "mesh", [(m, m ^ 2) for m in range(mesh_count)])
 
     def sources(start, size, rims, after=()):
-        at_once = 3
-        pieces_in = [
-            pl.BlockSpec(
-                (2, at_once, 1, quarter, lanes),
-                functools.partial(lambda plane, b: (0, b, plane, 0, 0), start + p),
-            )
-            for _ in range(4)
-            for p in range(size)
-        ]
-        rim_specs = [
-            pl.BlockSpec((INST // 2, at_once, quarter, lanes), lambda b: (0, b, 0, 0)),
-            pl.BlockSpec((INST // 2, at_once, quarter, lanes), lambda b: (0, b, 0, 0)),
-            pl.BlockSpec((planes, rows, lanes), lambda b: (0, 0, 0)),
-        ]
+        at_once = 2
+
         def kernel(*refs):
             inputs, outputs = refs[: -4 - len(after)], refs[-4:]
-            source_kernel(bool(rims), *inputs, *outputs)
+            source_kernel(bool(rims), start, *inputs, *outputs)
 
         outs = pl.pallas_call(
             kernel,
             out_shape=(pltpu.HBM((*split, size, quarter, lanes), jnp.float32),) * 4,
             grid=(variables // at_once,),
-            in_specs=[SMEM] + pieces_in + rim_specs[: len(rims)] + [ANY] * len(after),
+            in_specs=[
+                SMEM,
+                pl.BlockSpec((2, at_once, planes, quarter, lanes), lambda b: (0, b, 0, 0, 0)),
+            ]
+            + [VMEM] * (3 + len(rims))
+            + [ANY] * len(after),
             out_specs=(
                 pl.BlockSpec((2, at_once, size, quarter, lanes), lambda b: (0, b, 0, 0, 0)),
             )
             * 4,
             compiler_params=params(),
             cost_estimate=cost(),
-        )(ratio[None], *(x for x in all_quarters for _ in range(size)), *rims, *after)
+        )(ratio[None], *all_quarters, *rims, *after)
         own, up, down, far = (x.reshape(blocks, size, quarter, lanes) for x in outs)
         return (own, *exchange(up, down, far))
 
@@ -463,13 +463,17 @@
     turn = jnp.where(first, angle, -angle)
     ghost_shape = shaped(INST // 2, variables, quarter, lanes)
 
-    outermost = pl.BlockSpec((2, variables, 2, quarter, lanes), lambda b: (0, 0, 3, 0, 0))
     ghost_out = pl.pallas_call(
         mix_kernel,
         out_shape=(ghost_shape,) * 2,
         grid=(1,),
-        in_specs=[SMEM] + [outermost] * 4 + [ANY],
-        out_specs=(pl.BlockSpec(ghost_shape.shape, lambda b: (0, 0, 0, 0)),) * 2,
+        in_specs=[
+            SMEM,
+            pl.BlockSpec((2, variables, 2, quarter, lanes), lambda b: (0, 0, planes // 2 - 1, 0, 0)),
+        ]
+        + [VMEM] * 3
+        + [ANY],
+        out_specs=(VMEM,) * 2,
         compiler_params=params(),
         cost_estimate=cost(),
     )(
@@ -514,7 +518,7 @@
         given = 4 + len(group)
         near = size < 4
         if near:
-            group = [pltpu.with_memory_space_constraint(x, pltpu.VMEM) for x in group]
+            group = in_vmem(*group)
             given_in = (pre, *group)
         else:
             given_in = (*in_hbm(pre, group[0]), *group[1:])

time: 89.9 us -> 92.1 us (1.024)
  Pallas kernels: 30.1 us -> 33.3 us
  waiting for transfers between devices: 23.7 us -> 22.2 us
    pallas_call x2, Pallas kernels: 5.07 us -> 7.8 us  [sources(): pl.pallas_call(kernel, out_shape=(pltpu.HBM((*split, size, quarter, lanes...]
  transfers between devices with their start and end apart: 18 -> 18, of which waited for: 9 -> 9; matrix products, arithmetic and copies ran while one was open for 3% -> 4% of each run, Pallas kernels for 24% -> 26%
where the time goes in v1:
time: 92.1 us; the launch traced here: 91.3 us
  Pallas kernels  33.3 us (36%)
  starting transfers between devices  27.6 us (30%)
  waiting for transfers between devices  22.2 us (24%)
  local copies, waits for them, and re-layouts  3.13 us (3%)
  between operations  3 us (3%)
  other arithmetic  2.06 us (2%)
    ppermute x9, waiting for transfers between devices, along(): return lax.ppermute(x, 'inst', [(j, (j + step) % 4) for j in range(4)])  9.95 us
    ppermute x9, starting transfers between devices, along(): return lax.ppermute(x, 'inst', [(j, (j + step) % 4) for j in range(4)])  9.64 us
    pallas_call x2, Pallas kernels, sources(): pl.pallas_call(kernel, out_shape=(pltpu.HBM((*split, size, quarter, lanes...  7.8 us
    pallas_call x2, Pallas kernels, local(): pl.pallas_call(functools.partial(final_kernel, start, 4 if near else 2, n...  7.38 us
    ppermute x1, starting transfers between devices, local(): lax.ppermute(harmonics, 'mesh', [(m, m ^ 8) for m in range(mesh_count)])  5.85 us
    pallas_call x1, Pallas kernels, local(): pl.pallas_call(stencil_kernel, grid=(blocks // at_once,), out_shape=(pltp...  5.57 us
    ppermute x1, waiting for transfers between devices, local(): lax.ppermute(harmonics, 'mesh', [(m, m ^ 8) for m in range(mesh_count)])  4.7 us
    ppermute x1, waiting for transfers between devices, doubled(): lax.ppermute(x, 'mesh', [(m, m ^ flip) for m in range(mesh_count)])  4.56 us
  transfers between devices with their start and end apart: 18, of which 9 were waited for; matrix products, arithmetic and copies ran while one was open for 4% of the time, Pallas kernels for 26%

profile of v1, /device:TPU:97, one launch (start us, length us, event | category | flops | bytes accessed | tf_op | source)
XLA Modules:
  0.0 91.3 jit_solution(12993465598023309213)
XLA Ops:
  0.7 3.6 %shard_map.68 = (f32[12,8,16,128]{3,2,1,0:T(8,128)}, f32[12,8,16,128]{3,2,1,0:T(8,128)}, f32[12,8,16,128]{3,2,1,0:T(8,128)}) custom-call(f32[12,8,64,128]{3,2,1,0:T(8,128)} %bitcast.20), custom_call_target="tpu_custom_call" | custom-call | flops 1 | bytes 1 | tf_op jit(solution)/shard_map/pallas_call | solution.py:103
  4.2 2.5 %collective-permute-start.3 = (f32[12,8,16,128]{3,2,1,0:T(8,128)}, f32[12,8,16,128]{3,2,1,0:T(8,128)}, u32[]{:S(2)}, u32[]{:S(2)}) collective-permute-start(f32[12,8,16,128]{3,2,1,0:T(8,128)} %get-tuple-element.26), channel_id=1, source_target_pairs={{0,48},{16,0},{32,16},{48,32},{1,49},{17,1},{33,17},{49,33},{2,50}... | collective-permute-start | bytes 2359304 | tf_op jit(solution)/shard_map/ppermute | solution.py:353
  7.9 1.6 %shard_map.69 = f32[24,1536]{1,0:T(8,128)S(1)} custom-call(s32[8]{0:T(128)S(1)} %copy-done.7, f32[12,8,16,128]{3,2,1,0:T(8,128)} %get-tuple-element.24.after, f32[12,8,64,128]{3,2,1,0:T(8,128)S(1)} %bitcast.22, f32[12,8,64,128]{3,2,1,0:T(8,128)S(1)} %bitcast.23), custom_call_target="tpu_custom_call" | custom-call | flops 1 | bytes 1 | tf_op jit(solution)/shard_map/pallas_call | solution.py:404
  9.6 4.4 %collective-permute-start.1 = (f32[24,1536]{1,0:T(8,128)S(1)}, f32[24,1536]{1,0:T(8,128)S(1)}, u32[]{:S(2)}, u32[]{:S(2)}) collective-permute-start(f32[24,1536]{1,0:T(8,128)S(1)} %shard_map.69), channel_id=1, source_target_pairs={{0,65},{1,64},{2,67},{3,66},{4,69},{5,68},{6,71},{7,70},{8,73},{9,... | collective-permute-start | bytes 442376 | tf_op jit(solution)/shard_map/ppermute | solution.py:429
  14.0 3.7 %shard_map.70 = (f32[12,64,128]{2,1,0:T(8,128)S(1)}, f32[12,64,128]{2,1,0:T(8,128)}, f32[12,8,16,128]{3,2,1,0:T(8,128)S(1)}) custom-call(f32[12,8,64,128]{3,2,1,0:T(8,128)} %bitcast.21, f32[12,8,16,128]{3,2,1,0:T(8,128)} %get-tuple-element.24.after), custom_call_target="tpu_custom_call" | custom-call | flops 1 | bytes 1 | tf_op jit(solution)/shard_map/pallas_call | solution.py:368
  18.7 1.9 %collective-permute-start.6 = (f32[12,64,128]{2,1,0:T(8,128)S(1)}, f32[12,64,128]{2,1,0:T(8,128)S(1)}, u32[]{:S(2)}, u32[]{:S(2)}) collective-permute-start(f32[12,64,128]{2,1,0:T(8,128)S(1)} %get-tuple-element.28), channel_id=1, source_target_pairs={{0,1},{1,2},{2,3},{3,4},{4,5},{5,6},{6,7},{7,8},{8,9},{9,10},{10,1... | collective-permute-start | bytes 1179656 | tf_op jit(solution)/shard_map/ppermute | solution.py:377
  21.5 2.4 %collective-permute-start.7 = (f32[12,64,128]{2,1,0:T(8,128)}, f32[12,64,128]{2,1,0:T(8,128)}, u32[]{:S(2)}, u32[]{:S(2)}) collective-permute-start(f32[12,64,128]{2,1,0:T(8,128)} %get-tuple-element.29), channel_id=1, source_target_pairs={{1,0},{2,1},{3,2},{4,3},{5,4},{6,5},{7,6},{8,7},{9,8},{10,9},{11,1... | collective-permute-start | bytes 1179656 | tf_op jit(solution)/shard_map/ppermute | solution.py:378
  26.1 1.7 %collective-permute-start.2 = (f32[24,1536]{1,0:T(8,128)}, f32[24,1536]{1,0:T(8,128)S(1)}, u32[]{:S(2)}, u32[]{:S(2)}) collective-permute-start(f32[24,1536]{1,0:T(8,128)} %add.26.one), channel_id=1, source_target_pairs={{0,2},{1,3},{2,0},{3,1},{4,6},{5,7},{6,4},{7,5},{8,10},{9,11},{10,... | collective-permute-start | bytes 442376 | tf_op jit(solution)/shard_map/ppermute | solution.py:431
  29.0 1.4 %fusion = (f32[1]{0:T(128)}, f32[1]{0:T(128)}) fusion(f32[2]{0:T(128)} %convert_element_type.7, s32[]{:T(128)S(6)} %select_n.14, s32[]{:T(128)S(6)} %select_n.15), kind=kLoop, calls=%fused_computation.2 | loop fusion | bytes 24 | tf_op jit(solution)/shard_map/dynamic_slice | solution.py:345
  31.8 1.2 %collective-permute-done.7.high = f32[12,64,128]{2,1,0:T(8,128)} collective-permute-done((f32[12,64,128]{2,1,0:T(8,128)}, f32[12,64,128]{2,1,0:T(8,128)}, u32[]{:S(2)}, u32[]{:S(2)}) %collective-permute-start.7) | collective-permute-done | bytes 393248 | tf_op jit(solution)/shard_map/ppermute | solution.py:378
  33.0 5.6 %shard_map.71 = (f32[12,6,64,128]{3,2,1,0:T(8,128)}, f32[12,2,64,128]{3,2,1,0:T(8,128)}) custom-call(f32[8,64,128]{2,1,0:T(8,128)S(1)} %bitcast.30, f32[12,64,128]{2,1,0:T(8,128)} %copy-done.9, f32[12,64,128]{2,1,0:T(8,128)} %collective-permute-done.7.high, f32[12,8,64,128]{3,2,1,0:T(8,128)S(1)} %bitcast.24), custom_call_target="tpu_custom_call" | custom-call | flops 1 | bytes 1 | tf_op jit(solution)/shard_map/pallas_call | solution.py:388
  38.6 6.3 %collective-permute-done.4 = f32[12,8,16,128]{3,2,1,0:T(8,128)} collective-permute-done((f32[12,8,16,128]{3,2,1,0:T(8,128)}, f32[12,8,16,128]{3,2,1,0:T(8,128)}, u32[]{:S(2)}, u32[]{:S(2)}) %collective-permute-start.4) | collective-permute-done | bytes 786464 | tf_op jit(solution)/shard_map/ppermute | solution.py:353
  44.9 4.1 %shard_map.72 = (f32[2,6,6,16,128]{4,3,2,1,0:T(8,128)}, f32[2,6,6,16,128]{4,3,2,1,0:T(8,128)}, f32[2,6,6,16,128]{4,3,2,1,0:T(8,128)}, f32[2,6,6,16,128]{4,3,2,1,0:T(8,128)}) custom-call(f32[1]{0:T(128)} %div.15.refs_0_, f32[2,6,8,16,128]{4,3,2,1,0:T(8,128)} %bitcast.27, f32[2,6,8,16,128]{4,3,2,1,0:T(8,128)} %bitcast.6.refs_2_.up, ...), custom_call_target="tpu_custom_call" | custom-call | flops 1 | bytes 1 | tf_op jit(solution)/shard_map/pallas_call | solution.py:440
  49.9 1.5 %collective-permute-start.11 = (f32[12,6,16,128]{3,2,1,0:T(8,128)}, f32[12,6,16,128]{3,2,1,0:T(8,128)S(1)}, u32[]{:S(2)}, u32[]{:S(2)}) collective-permute-start(f32[12,6,16,128]{3,2,1,0:T(8,128)} %bitcast.39), channel_id=1, source_target_pairs={{0,16},{16,32},{32,48},{48,0},{1,17},{17,33},{33,49},{49,1},{2,18}... | collective-permute-start | bytes 1769480 | tf_op jit(solution)/shard_map/ppermute | solution.py:353
  52.1 1.9 %shard_map.73 = (f32[4,6,16,128]{3,2,1,0:T(8,128)S(1)}, f32[4,6,16,128]{3,2,1,0:T(8,128)S(1)}) custom-call(f32[10]{0:T(128)S(1)} %pad_maximum_fusion.scalars, f32[2,6,8,16,128]{4,3,2,1,0:T(8,128)} %bitcast.28, f32[2,6,8,16,128]{4,3,2,1,0:T(8,128)} %bitcast.6.refs_2_.up, f32[2,6,8,16,128]{4,3,2,1,0:T(8,128)} %bitcast.7.refs_3_.down, ...), custom_call_target="tpu_custom_call" | custom-call | flops 1 | bytes 1 | tf_op jit(solution)/shard_map/pallas_call | solution.py:466
  56.0 4.6 %collective-permute-done.8 = f32[24,1536]{1,0:T(8,128)S(1)} collective-permute-done((f32[24,1536]{1,0:T(8,128)S(1)}, f32[24,1536]{1,0:T(8,128)S(1)}, u32[]{:S(2)}, u32[]{:S(2)}) %collective-permute-start.8) | collective-permute-done | bytes 147488 | tf_op jit(solution)/shard_map/ppermute | solution.py:427
  61.2 5.9 %collective-permute-start.9 = (f32[24,1536]{1,0:T(8,128)S(1)}, f32[24,1536]{1,0:T(8,128)S(1)}, u32[]{:S(2)}, u32[]{:S(2)}) collective-permute-start(f32[24,1536]{1,0:T(8,128)S(1)} %add.33.one), channel_id=1, source_target_pairs={{0,8},{1,9},{2,10},{3,11},{4,12},{5,13},{6,14},{7,15},{8,0},{9,1},... | collective-permute-start | bytes 442376 | tf_op jit(solution)/shard_map/ppermute | solution.py:497
  67.1 4.7 %collective-permute-done.9.two.refs_8_ = f32[24,1536]{1,0:T(8,128)S(1)} collective-permute-done((f32[24,1536]{1,0:T(8,128)S(1)}, f32[24,1536]{1,0:T(8,128)S(1)}, u32[]{:S(2)}, u32[]{:S(2)}) %collective-permute-start.9) | collective-permute-done | bytes 147488 | tf_op jit(solution)/shard_map/ppermute | solution.py:497
  71.8 3.7 %shard_map.76 = (f32[2,6,2,16,128]{4,3,2,1,0:T(8,128)}, f32[2,6,2,16,128]{4,3,2,1,0:T(8,128)}, f32[2,6,2,16,128]{4,3,2,1,0:T(8,128)}, f32[2,6,2,16,128]{4,3,2,1,0:T(8,128)}) custom-call(f32[1]{0:T(128)} %div.15.refs_0_, f32[2,6,8,16,128]{4,3,2,1,0:T(8,128)} %bitcast.29, f32[2,6,8,16,128]{4,3,2,1,0:T(8,128)} %bitcast.6.refs_2_.up, ...), custom_call_target="tpu_custom_call" | custom-call | flops 1 | bytes 1 | tf_op jit(solution)/shard_map/pallas_call | solution.py:440
  75.5 2.0 %collective-permute-start.15 = (f32[12,2,16,128]{3,2,1,0:T(8,128)}, f32[12,2,16,128]{3,2,1,0:T(8,128)S(1)}, u32[]{:S(2)}, u32[]{:S(2)}) collective-permute-start(f32[12,2,16,128]{3,2,1,0:T(8,128)} %bitcast.43), channel_id=1, source_target_pairs={{0,48},{16,0},{32,16},{48,32},{1,49},{17,1},{33,17},{49,33},{2,50}... | collective-permute-start | bytes 589832 | tf_op jit(solution)/shard_map/ppermute | solution.py:353
  77.5 1.9 %collective-permute-start.17 = (f32[12,2,16,128]{3,2,1,0:T(8,128)}, f32[12,2,16,128]{3,2,1,0:T(8,128)S(1)}, u32[]{:S(2)}, u32[]{:S(2)}) collective-permute-start(f32[12,2,16,128]{3,2,1,0:T(8,128)} %bitcast.41), channel_id=1, source_target_pairs={{0,32},{16,48},{32,0},{48,16},{1,33},{17,49},{33,1},{49,17},{2,34}... | collective-permute-start | bytes 589832 | tf_op jit(solution)/shard_map/ppermute | solution.py:353
  80.3 5.0 %shard_map.77 = (f32[12,8,64,128]{3,2,1,0:T(8,128)}, f32[12,8,64,128]{3,2,1,0:T(8,128)}) custom-call(bf16[64,192]{1,0:T(8,128)(2,1)S(1)} %copy-done.6, f32[8,12,8,128]{3,2,1,0:T(8,128)S(1)} %shard_map.75.edge, f32[12,8,64,128]{3,2,1,0:T(8,128)S(1)} %bitcast.25, f32[12,6,64,128]{3,2,1,0:T(8,128)} %get-tuple-element.30.refs_5_.pre, ...), custom_call_target="tpu_custom_call" | custom-call | flops 1 | bytes 1 | tf_op jit(solution)/shard_map/pallas_call | solution.py:525
  85.7 3.3 %collective-permute-done.16.rest_2_ = f32[12,2,16,128]{3,2,1,0:T(8,128)S(1)} collective-permute-done((f32[12,2,16,128]{3,2,1,0:T(8,128)}, f32[12,2,16,128]{3,2,1,0:T(8,128)S(1)}, u32[]{:S(2)}, u32[]{:S(2)}) %collective-permute-start.16) | collective-permute-done | bytes 196640 | tf_op jit(solution)/shard_map/ppermute | solution.py:353
  89.0 2.3 %shard_map.78 = (f32[12,8,64,128]{3,2,1,0:T(8,128)}, f32[12,8,64,128]{3,2,1,0:T(8,128)}) custom-call(bf16[64,192]{1,0:T(8,128)(2,1)S(1)} %copy-done.6, f32[8,12,8,128]{3,2,1,0:T(8,128)S(1)} %shard_map.75.edge, f32[12,8,64,128]{3,2,1,0:T(8,128)S(1)} %bitcast.26, f32[12,2,64,128]{3,2,1,0:T(8,128)S(1)} %copy-done.4, ...), custom_call_target="tpu_custom_call", output_to_operand_aliasing={{0}: (8, {}), {1}: (9, {})} | custom-call | flops 1 | bytes 1 | tf_op jit(solution)/shard_map/pallas_call | solution.py:525
  (49 shorter events, 11.1 us)
Async XLA Ops:
  4.2 34.4 %collective-permute-start.3 = (f32[12,8,16,128]{3,2,1,0:T(8,128)}, f32[12,8,16,128]{3,2,1,0:T(8,128)}, u32[]{:S(2)}, u32[]{:S(2)}) collective-permute-start(f32[12,8,16,128]{3,2,1,0:T(8,128)} %get-tuple-element.26), channel_id=1, source_target_pairs={{0,48},{16,0},{32,16},{48,32},{1,49},{17,1},{33,17},{49,33},{2,50}... | collective-permute-start | bytes 2359304 | tf_op jit(solution)/shard_map/ppermute | solution.py:353
  6.8 31.8 %collective-permute-start.5 = (f32[12,8,16,128]{3,2,1,0:T(8,128)}, f32[12,8,16,128]{3,2,1,0:T(8,128)}, u32[]{:S(2)}, u32[]{:S(2)}) collective-permute-start(f32[12,8,16,128]{3,2,1,0:T(8,128)} %get-tuple-element.27), channel_id=1, source_target_pairs={{0,32},{16,48},{32,0},{48,16},{1,33},{17,49},{33,1},{49,17},{2,34}... | collective-permute-start | bytes 2359304 | tf_op jit(solution)/shard_map/ppermute | solution.py:353
  7.3 37.6 %collective-permute-start.4 = (f32[12,8,16,128]{3,2,1,0:T(8,128)}, f32[12,8,16,128]{3,2,1,0:T(8,128)}, u32[]{:S(2)}, u32[]{:S(2)}) collective-permute-start(f32[12,8,16,128]{3,2,1,0:T(8,128)} %get-tuple-element.24.after), channel_id=1, source_target_pairs={{0,16},{16,32},{32,48},{48,0},{1,17},{17,33},{33,49},{49,1},{2,18}... | collective-permute-start | bytes 2359304 | tf_op jit(solution)/shard_map/ppermute | solution.py:353
  9.5 23.4 %copy-start.1 = (f32[1,2,6,8,64,128]{5,4,3,2,1,0:T(8,128)S(1)}, f32[1,2,6,8,64,128]{5,4,3,2,1,0:T(8,128)}, u32[]{:S(2)}) copy-start(f32[1,2,6,8,64,128]{5,4,3,2,1,0:T(8,128)} %param.5) | copy-start | bytes 9437188
  9.6 23.4 %copy-start.3 = (f32[1,8,64,128]{3,2,1,0:T(8,128)S(1)}, f32[1,8,64,128]{3,2,1,0:T(8,128)}, u32[]{:S(2)}) copy-start(f32[1,8,64,128]{3,2,1,0:T(8,128)} %param.6) | copy-start | bytes 786436
  9.6 9.1 %collective-permute-start.1 = (f32[24,1536]{1,0:T(8,128)S(1)}, f32[24,1536]{1,0:T(8,128)S(1)}, u32[]{:S(2)}, u32[]{:S(2)}) collective-permute-start(f32[24,1536]{1,0:T(8,128)S(1)} %shard_map.69), channel_id=1, source_target_pairs={{0,65},{1,64},{2,67},{3,66},{4,69},{5,68},{6,71},{7,70},{8,73},{9,... | collective-permute-start | bytes 442376 | tf_op jit(solution)/shard_map/ppermute | solution.py:429
  13.9 7.5 %collective-permute-start = (f32[24,1536]{1,0:T(8,128)S(1)}, f32[24,1536]{1,0:T(8,128)S(1)}, u32[]{:S(2)}, u32[]{:S(2)}) collective-permute-start(f32[24,1536]{1,0:T(8,128)S(1)} %shard_map.69), channel_id=1, source_target_pairs={{0,64},{1,65},{2,66},{3,67},{4,68},{5,69},{6,70},{7,71},{8,72},{9,... | collective-permute-start | bytes 442376 | tf_op jit(solution)/shard_map/ppermute | solution.py:429
  18.7 6.6 %collective-permute-start.6 = (f32[12,64,128]{2,1,0:T(8,128)S(1)}, f32[12,64,128]{2,1,0:T(8,128)S(1)}, u32[]{:S(2)}, u32[]{:S(2)}) collective-permute-start(f32[12,64,128]{2,1,0:T(8,128)S(1)} %get-tuple-element.28), channel_id=1, source_target_pairs={{0,1},{1,2},{2,3},{3,4},{4,5},{5,6},{6,7},{7,8},{8,9},{9,10},{10,1... | collective-permute-start | bytes 1179656 | tf_op jit(solution)/shard_map/ppermute | solution.py:377
  21.5 11.5 %collective-permute-start.7 = (f32[12,64,128]{2,1,0:T(8,128)}, f32[12,64,128]{2,1,0:T(8,128)}, u32[]{:S(2)}, u32[]{:S(2)}) collective-permute-start(f32[12,64,128]{2,1,0:T(8,128)} %get-tuple-element.29), channel_id=1, source_target_pairs={{1,0},{2,1},{3,2},{4,3},{5,4},{6,5},{7,6},{8,7},{9,8},{10,9},{11,1... | collective-permute-start | bytes 1179656 | tf_op jit(solution)/shard_map/ppermute | solution.py:378
  26.1 12.5 %collective-permute-start.2 = (f32[24,1536]{1,0:T(8,128)}, f32[24,1536]{1,0:T(8,128)S(1)}, u32[]{:S(2)}, u32[]{:S(2)}) collective-permute-start(f32[24,1536]{1,0:T(8,128)} %add.26.one), channel_id=1, source_target_pairs={{0,2},{1,3},{2,0},{3,1},{4,6},{5,7},{6,4},{7,5},{8,10},{9,11},{10,... | collective-permute-start | bytes 442376 | tf_op jit(solution)/shard_map/ppermute | solution.py:431
  49.0 28.5 %collective-permute-start.10 = (f32[12,6,16,128]{3,2,1,0:T(8,128)}, f32[12,6,16,128]{3,2,1,0:T(8,128)}, u32[]{:S(2)}, u32[]{:S(2)}) collective-permute-start(f32[12,6,16,128]{3,2,1,0:T(8,128)} %bitcast.40), channel_id=1, source_target_pairs={{0,48},{16,0},{32,16},{48,32},{1,49},{17,1},{33,17},{49,33},{2,50}... | collective-permute-start | bytes 1769480 | tf_op jit(solution)/shard_map/ppermute | solution.py:353
  49.9 29.5 %collective-permute-start.11 = (f32[12,6,16,128]{3,2,1,0:T(8,128)}, f32[12,6,16,128]{3,2,1,0:T(8,128)S(1)}, u32[]{:S(2)}, u32[]{:S(2)}) collective-permute-start(f32[12,6,16,128]{3,2,1,0:T(8,128)} %bitcast.39), channel_id=1, source_target_pairs={{0,16},{16,32},{32,48},{48,0},{1,17},{17,33},{33,49},{49,1},{2,18}... | collective-permute-start | bytes 1769480 | tf_op jit(solution)/shard_map/ppermute | solution.py:353
  51.5 28.0 %collective-permute-start.12 = (f32[12,6,16,128]{3,2,1,0:T(8,128)}, f32[12,6,16,128]{3,2,1,0:T(8,128)S(1)}, u32[]{:S(2)}, u32[]{:S(2)}) collective-permute-start(f32[12,6,16,128]{3,2,1,0:T(8,128)} %bitcast.38), channel_id=1, source_target_pairs={{0,32},{16,48},{32,0},{48,16},{1,33},{17,49},{33,1},{49,17},{2,34}... | collective-permute-start | bytes 1769480 | tf_op jit(solution)/shard_map/ppermute | solution.py:353
  54.0 25.4 %copy-start.8 = (s32[8]{0:T(128)S(1)}, s32[8]{0:T(128)}, u32[]{:S(2)}) copy-start(s32[8]{0:T(128)} %orders.3) | copy-start | bytes 100
  55.0 5.6 %collective-permute-start.8 = (f32[24,1536]{1,0:T(8,128)S(1)}, f32[24,1536]{1,0:T(8,128)S(1)}, u32[]{:S(2)}, u32[]{:S(2)}) collective-permute-start(f32[24,1536]{1,0:T(8,128)S(1)} %shard_map.74), channel_id=1, source_target_pairs={{0,4},{1,5},{2,6},{3,7},{4,0},{5,1},{6,2},{7,3},{8,12},{9,13},{10,... | collective-permute-start | bytes 442376 | tf_op jit(solution)/shard_map/ppermute | solution.py:427
  55.3 5.9 %collective-permute-start.14 = (f32[4,6,16,128]{3,2,1,0:T(8,128)S(1)}, f32[4,6,16,128]{3,2,1,0:T(8,128)S(1)}, u32[]{:S(2)}, u32[]{:S(2)}) collective-permute-start(f32[4,6,16,128]{3,2,1,0:T(8,128)S(1)} %get-tuple-element.37), channel_id=1, source_target_pairs={{15,0},{0,15},{31,16},{16,31},{47,32},{32,47},{63,48},{48,63},{79,... | collective-permute-start | bytes 589832 | tf_op jit(solution)/shard_map/ppermute | solution.py:485
  60.5 6.6 %collective-permute-start.13 = (f32[4,6,16,128]{3,2,1,0:T(8,128)S(1)}, f32[4,6,16,128]{3,2,1,0:T(8,128)S(1)}, u32[]{:S(2)}, u32[]{:S(2)}) collective-permute-start(f32[4,6,16,128]{3,2,1,0:T(8,128)S(1)} %get-tuple-element.32.after), channel_id=1, source_target_pairs={{15,0},{0,15},{31,16},{16,31},{47,32},{32,47},{63,48},{48,63},{79,... | collective-permute-start | bytes 589832 | tf_op jit(solution)/shard_map/ppermute | solution.py:485
  61.2 19.1 %copy-start.6 = (bf16[64,192]{1,0:T(8,128)(2,1)S(1)}, bf16[64,192]{1,0:T(8,128)(2,1)}, u32[]{:S(2)}) copy-start(bf16[64,192]{1,0:T(8,128)(2,1)} %constant.38.clone.inverse) | copy-start | bytes 73732
  61.2 10.6 %collective-permute-start.9 = (f32[24,1536]{1,0:T(8,128)S(1)}, f32[24,1536]{1,0:T(8,128)S(1)}, u32[]{:S(2)}, u32[]{:S(2)}) collective-permute-start(f32[24,1536]{1,0:T(8,128)S(1)} %add.33.one), channel_id=1, source_target_pairs={{0,8},{1,9},{2,10},{3,11},{4,12},{5,13},{6,14},{7,15},{8,0},{9,1},... | collective-permute-start | bytes 442376 | tf_op jit(solution)/shard_map/ppermute | solution.py:497
  75.5 10.2 %collective-permute-start.15 = (f32[12,2,16,128]{3,2,1,0:T(8,128)}, f32[12,2,16,128]{3,2,1,0:T(8,128)S(1)}, u32[]{:S(2)}, u32[]{:S(2)}) collective-permute-start(f32[12,2,16,128]{3,2,1,0:T(8,128)} %bitcast.43), channel_id=1, source_target_pairs={{0,48},{16,0},{32,16},{48,32},{1,49},{17,1},{33,17},{49,33},{2,50}... | collective-permute-start | bytes 589832 | tf_op jit(solution)/shard_map/ppermute | solution.py:353
  77.5 11.5 %collective-permute-start.16 = (f32[12,2,16,128]{3,2,1,0:T(8,128)}, f32[12,2,16,128]{3,2,1,0:T(8,128)S(1)}, u32[]{:S(2)}, u32[]{:S(2)}) collective-permute-start(f32[12,2,16,128]{3,2,1,0:T(8,128)} %bitcast.42), channel_id=1, source_target_pairs={{0,16},{16,32},{32,48},{48,0},{1,17},{17,33},{33,49},{49,1},{2,18}... | collective-permute-start | bytes 589832 | tf_op jit(solution)/shard_map/ppermute | solution.py:353
  77.5 11.5 %collective-permute-start.17 = (f32[12,2,16,128]{3,2,1,0:T(8,128)}, f32[12,2,16,128]{3,2,1,0:T(8,128)S(1)}, u32[]{:S(2)}, u32[]{:S(2)}) collective-permute-start(f32[12,2,16,128]{3,2,1,0:T(8,128)} %bitcast.41), channel_id=1, source_target_pairs={{0,32},{16,48},{32,0},{48,16},{1,33},{17,49},{33,1},{49,17},{2,34}... | collective-permute-start | bytes 589832 | tf_op jit(solution)/shard_map/ppermute | solution.py:353
  80.3 8.7 %copy-start.4 = (f32[12,2,64,128]{3,2,1,0:T(8,128)S(1)}, f32[12,2,64,128]{3,2,1,0:T(8,128)}, u32[]{:S(2)}) copy-start(f32[12,2,64,128]{3,2,1,0:T(8,128)} %get-tuple-element.36.pre) | copy-start | bytes 2359300
  80.3 8.7 %copy-start.5 = (f32[2,6,2,16,128]{4,3,2,1,0:T(8,128)S(1)}, f32[2,6,2,16,128]{4,3,2,1,0:T(8,128)}, u32[]{:S(2)}) copy-start(f32[2,6,2,16,128]{4,3,2,1,0:T(8,128)} %get-tuple-element.38) | copy-start | bytes 589828
  (4 other events, 16.3 us)

commit v2 on v0

--- a/solution.py
+++ b/solution.py
@@ -167,16 +167,15 @@
     if rims:
         *ghost, nu = refs[-3:]
         refs = refs[:-3]
-    size = len(refs) // 4
-    own, up, down, far = (refs[k * size : (k + 1) * size] for k in range(4))
+    own, up, down, far = refs
+    size = up.shape[2]
     ratio = scalars[0]
     c1, c2, c3 = (ratio * D1, ratio * D2, ratio * D3)
     out_own, out_up, out_down, out_far = outs
     order = (out_own, out_up, out_far, out_down)
-    for var in range(up[0].shape[1]):
+    for var in range(up.shape[1]):
         for p in range(size):
-            u = [own[p][s, var, 0] for s in range(2)]
-            u += [r[p][s, var, 0] for r in (up, far, down) for s in range(2)]
+            u = [r[s, var, p] for r in (own, up, far, down) for s in range(2)]
             near = [u[(n - 1) % INST] - u[(n + 1) % INST] for n in range(INST)]
             second = [c2 * (u[(n - 2) % INST] - u[(n + 2) % INST]) for n in range(4)]
             for n in range(INST):
@@ -187,7 +186,7 @@
         return
 
     def add_ghost(p, factor):
-        for var in range(up[0].shape[1]):
+        for var in range(up.shape[1]):
             for n in range(INST):
                 at = (n % 2, var, p)
                 order[n // 2][at] = order[n // 2][at] - factor * ghost[n // 4][n % 4, var]
@@ -425,14 +424,9 @@
 
     def sources(start, size, rims, after=()):
         at_once = 3
-        pieces_in = [
-            pl.BlockSpec(
-                (2, at_once, 1, quarter, lanes),
-                functools.partial(lambda plane, b: (0, b, plane, 0, 0), start + p),
-            )
-            for _ in range(4)
-            for p in range(size)
-        ]
+        piece_in = pl.BlockSpec(
+            (2, at_once, size, quarter, lanes), lambda b: (0, b, start // size, 0, 0)
+        )
         rim_specs = [
             pl.BlockSpec((INST // 2, at_once, quarter, lanes), lambda b: (0, b, 0, 0)),
             pl.BlockSpec((INST // 2, at_once, quarter, lanes), lambda b: (0, b, 0, 0)),
@@ -446,14 +440,14 @@
             kernel,
             out_shape=(pltpu.HBM((*split, size, quarter, lanes), jnp.float32),) * 4,
             grid=(variables // at_once,),
-            in_specs=[SMEM] + pieces_in + rim_specs[: len(rims)] + [ANY] * len(after),
+            in_specs=[SMEM] + [piece_in] * 4 + rim_specs[: len(rims)] + [ANY] * len(after),
             out_specs=(
                 pl.BlockSpec((2, at_once, size, quarter, lanes), lambda b: (0, b, 0, 0, 0)),
             )
             * 4,
             compiler_params=params(),
             cost_estimate=cost(),
-        )(ratio[None], *(x for x in all_quarters for _ in range(size)), *rims, *after)
+        )(ratio[None], *all_quarters, *rims, *after)
         own, up, down, far = (x.reshape(blocks, size, quarter, lanes) for x in outs)
         return (own, *exchange(up, down, far))
 

time: 89.9 us -> 89.5 us (level)
  transfers between devices with their start and end apart: 18 -> 18, of which waited for: 9 -> 9; matrix products, arithmetic and copies ran while one was open for 3% -> 4% of each run, Pallas kernels for 24% -> 24%
where the time goes in v2:
time: 89.5 us; the launch traced here: 88.8 us
  Pallas kernels  30 us (34%)
  starting transfers between devices  27.6 us (31%)
  waiting for transfers between devices  22.9 us (26%)
  local copies, waits for them, and re-layouts  3.13 us (3%)
  between operations  3 us (3%)
  other arithmetic  2.06 us (2%)
    ppermute x9, waiting for transfers between devices, along(): return lax.ppermute(x, 'inst', [(j, (j + step) % 4) for j in range(4)])  10.7 us
    ppermute x9, starting transfers between devices, along(): return lax.ppermute(x, 'inst', [(j, (j + step) % 4) for j in range(4)])  9.66 us
    pallas_call x2, Pallas kernels, local(): pl.pallas_call(functools.partial(final_kernel, start, 4 if near else 2, n...  7.38 us
    ppermute x1, starting transfers between devices, local(): lax.ppermute(harmonics, 'mesh', [(m, m ^ 8) for m in range(mesh_count)])  5.85 us
    pallas_call x1, Pallas kernels, local(): pl.pallas_call(stencil_kernel, grid=(blocks // at_once,), out_shape=(pltp...  5.57 us
    pallas_call x2, Pallas kernels, sources(): pl.pallas_call(kernel, out_shape=(pltpu.HBM((*split, size, quarter, lanes...  4.99 us
    ppermute x1, waiting for transfers between devices, local(): lax.ppermute(harmonics, 'mesh', [(m, m ^ 8) for m in range(mesh_count)])  4.7 us
    ppermute x1, waiting for transfers between devices, doubled(): lax.ppermute(x, 'mesh', [(m, m ^ flip) for m in range(mesh_count)])  4.56 us
  transfers between devices with their start and end apart: 18, of which 9 were waited for; matrix products, arithmetic and copies ran while one was open for 4% of the time, Pallas kernels for 24%

profile of v2, /device:TPU:97, one launch (start us, length us, event | category | flops | bytes accessed | tf_op | source)
XLA Modules:
  0.0 88.8 jit_solution(3190176718003549137)
XLA Ops:
  0.7 3.6 %shard_map.68 = (f32[12,8,16,128]{3,2,1,0:T(8,128)}, f32[12,8,16,128]{3,2,1,0:T(8,128)}, f32[12,8,16,128]{3,2,1,0:T(8,128)}) custom-call(f32[12,8,64,128]{3,2,1,0:T(8,128)} %bitcast.20), custom_call_target="tpu_custom_call" | custom-call | flops 1 | bytes 1 | tf_op jit(solution)/shard_map/pallas_call | solution.py:103
  4.2 2.5 %collective-permute-start.3 = (f32[12,8,16,128]{3,2,1,0:T(8,128)}, f32[12,8,16,128]{3,2,1,0:T(8,128)}, u32[]{:S(2)}, u32[]{:S(2)}) collective-permute-start(f32[12,8,16,128]{3,2,1,0:T(8,128)} %get-tuple-element.26), channel_id=1, source_target_pairs={{0,48},{16,0},{32,16},{48,32},{1,49},{17,1},{33,17},{49,33},{2,50}... | collective-permute-start | bytes 2359304 | tf_op jit(solution)/shard_map/ppermute | solution.py:349
  7.9 1.6 %shard_map.69 = f32[24,1536]{1,0:T(8,128)S(1)} custom-call(s32[8]{0:T(128)S(1)} %copy-done.7, f32[12,8,16,128]{3,2,1,0:T(8,128)} %get-tuple-element.24.after, f32[12,8,64,128]{3,2,1,0:T(8,128)S(1)} %bitcast.22, f32[12,8,64,128]{3,2,1,0:T(8,128)S(1)} %bitcast.23), custom_call_target="tpu_custom_call" | custom-call | flops 1 | bytes 1 | tf_op jit(solution)/shard_map/pallas_call | solution.py:396
  9.6 4.4 %collective-permute-start.1 = (f32[24,1536]{1,0:T(8,128)S(1)}, f32[24,1536]{1,0:T(8,128)S(1)}, u32[]{:S(2)}, u32[]{:S(2)}) collective-permute-start(f32[24,1536]{1,0:T(8,128)S(1)} %shard_map.69), channel_id=1, source_target_pairs={{0,65},{1,64},{2,67},{3,66},{4,69},{5,68},{6,71},{7,70},{8,73},{9,... | collective-permute-start | bytes 442376 | tf_op jit(solution)/shard_map/ppermute | solution.py:421
  14.0 3.7 %shard_map.70 = (f32[12,64,128]{2,1,0:T(8,128)S(1)}, f32[12,64,128]{2,1,0:T(8,128)}, f32[12,8,16,128]{3,2,1,0:T(8,128)S(1)}) custom-call(f32[12,8,64,128]{3,2,1,0:T(8,128)} %bitcast.21, f32[12,8,16,128]{3,2,1,0:T(8,128)} %get-tuple-element.24.after), custom_call_target="tpu_custom_call" | custom-call | flops 1 | bytes 1 | tf_op jit(solution)/shard_map/pallas_call | solution.py:361
  18.7 1.9 %collective-permute-start.6 = (f32[12,64,128]{2,1,0:T(8,128)S(1)}, f32[12,64,128]{2,1,0:T(8,128)S(1)}, u32[]{:S(2)}, u32[]{:S(2)}) collective-permute-start(f32[12,64,128]{2,1,0:T(8,128)S(1)} %get-tuple-element.28), channel_id=1, source_target_pairs={{0,1},{1,2},{2,3},{3,4},{4,5},{5,6},{6,7},{7,8},{8,9},{9,10},{10,1... | collective-permute-start | bytes 1179656 | tf_op jit(solution)/shard_map/ppermute | solution.py:370
  21.5 2.4 %collective-permute-start.7 = (f32[12,64,128]{2,1,0:T(8,128)}, f32[12,64,128]{2,1,0:T(8,128)}, u32[]{:S(2)}, u32[]{:S(2)}) collective-permute-start(f32[12,64,128]{2,1,0:T(8,128)} %get-tuple-element.29), channel_id=1, source_target_pairs={{1,0},{2,1},{3,2},{4,3},{5,4},{6,5},{7,6},{8,7},{9,8},{10,9},{11,1... | collective-permute-start | bytes 1179656 | tf_op jit(solution)/shard_map/ppermute | solution.py:371
  26.1 1.7 %collective-permute-start.2 = (f32[24,1536]{1,0:T(8,128)}, f32[24,1536]{1,0:T(8,128)S(1)}, u32[]{:S(2)}, u32[]{:S(2)}) collective-permute-start(f32[24,1536]{1,0:T(8,128)} %add.26.one), channel_id=1, source_target_pairs={{0,2},{1,3},{2,0},{3,1},{4,6},{5,7},{6,4},{7,5},{8,10},{9,11},{10,... | collective-permute-start | bytes 442376 | tf_op jit(solution)/shard_map/ppermute | solution.py:423
  29.0 1.4 %fusion = (f32[1]{0:T(128)}, f32[1]{0:T(128)}) fusion(f32[2]{0:T(128)} %convert_element_type.7, s32[]{:T(128)S(6)} %select_n.14, s32[]{:T(128)S(6)} %select_n.15), kind=kLoop, calls=%fused_computation.2 | loop fusion | bytes 24 | tf_op jit(solution)/shard_map/dynamic_slice | solution.py:341
  31.8 1.2 %collective-permute-done.7.high = f32[12,64,128]{2,1,0:T(8,128)} collective-permute-done((f32[12,64,128]{2,1,0:T(8,128)}, f32[12,64,128]{2,1,0:T(8,128)}, u32[]{:S(2)}, u32[]{:S(2)}) %collective-permute-start.7) | collective-permute-done | bytes 393248 | tf_op jit(solution)/shard_map/ppermute | solution.py:371
  33.0 5.6 %shard_map.71 = (f32[12,6,64,128]{3,2,1,0:T(8,128)}, f32[12,2,64,128]{3,2,1,0:T(8,128)}) custom-call(f32[8,64,128]{2,1,0:T(8,128)S(1)} %bitcast.30, f32[12,64,128]{2,1,0:T(8,128)} %copy-done.9, f32[12,64,128]{2,1,0:T(8,128)} %collective-permute-done.7.high, f32[12,8,64,128]{3,2,1,0:T(8,128)S(1)} %bitcast.24), custom_call_target="tpu_custom_call" | custom-call | flops 1 | bytes 1 | tf_op jit(solution)/shard_map/pallas_call | solution.py:380
  38.6 6.3 %collective-permute-done.4 = f32[12,8,16,128]{3,2,1,0:T(8,128)} collective-permute-done((f32[12,8,16,128]{3,2,1,0:T(8,128)}, f32[12,8,16,128]{3,2,1,0:T(8,128)}, u32[]{:S(2)}, u32[]{:S(2)}) %collective-permute-start.4) | collective-permute-done | bytes 786464 | tf_op jit(solution)/shard_map/ppermute | solution.py:349
  44.9 2.9 %shard_map.72 = (f32[2,6,6,16,128]{4,3,2,1,0:T(8,128)}, f32[2,6,6,16,128]{4,3,2,1,0:T(8,128)}, f32[2,6,6,16,128]{4,3,2,1,0:T(8,128)}, f32[2,6,6,16,128]{4,3,2,1,0:T(8,128)}) custom-call(f32[1]{0:T(128)} %div.15.refs_0_, f32[2,6,8,16,128]{4,3,2,1,0:T(8,128)} %bitcast.27, f32[2,6,8,16,128]{4,3,2,1,0:T(8,128)} %bitcast.6.refs_2_.up, ...), custom_call_target="tpu_custom_call" | custom-call | flops 1 | bytes 1 | tf_op jit(solution)/shard_map/pallas_call | solution.py:439
  48.7 1.5 %collective-permute-start.11 = (f32[12,6,16,128]{3,2,1,0:T(8,128)}, f32[12,6,16,128]{3,2,1,0:T(8,128)S(1)}, u32[]{:S(2)}, u32[]{:S(2)}) collective-permute-start(f32[12,6,16,128]{3,2,1,0:T(8,128)} %bitcast.39), channel_id=1, source_target_pairs={{0,16},{16,32},{32,48},{48,0},{1,17},{17,33},{33,49},{49,1},{2,18}... | collective-permute-start | bytes 1769480 | tf_op jit(solution)/shard_map/ppermute | solution.py:349
  50.8 1.4 %shard_map.73 = (f32[4,6,16,128]{3,2,1,0:T(8,128)S(1)}, f32[4,6,16,128]{3,2,1,0:T(8,128)S(1)}) custom-call(f32[10]{0:T(128)S(1)} %pad_maximum_fusion.scalars, f32[2,6,8,16,128]{4,3,2,1,0:T(8,128)} %bitcast.28, f32[2,6,8,16,128]{4,3,2,1,0:T(8,128)} %bitcast.6.refs_2_.up, f32[2,6,8,16,128]{4,3,2,1,0:T(8,128)} %bitcast.7.refs_3_.down, ...), custom_call_target="tpu_custom_call" | custom-call | flops 1 | bytes 1 | tf_op jit(solution)/shard_map/pallas_call | solution.py:461
  54.3 4.6 %collective-permute-done.8 = f32[24,1536]{1,0:T(8,128)S(1)} collective-permute-done((f32[24,1536]{1,0:T(8,128)S(1)}, f32[24,1536]{1,0:T(8,128)S(1)}, u32[]{:S(2)}, u32[]{:S(2)}) %collective-permute-start.8) | collective-permute-done | bytes 147488 | tf_op jit(solution)/shard_map/ppermute | solution.py:419
  59.5 5.9 %collective-permute-start.9 = (f32[24,1536]{1,0:T(8,128)S(1)}, f32[24,1536]{1,0:T(8,128)S(1)}, u32[]{:S(2)}, u32[]{:S(2)}) collective-permute-start(f32[24,1536]{1,0:T(8,128)S(1)} %add.33.one), channel_id=1, source_target_pairs={{0,8},{1,9},{2,10},{3,11},{4,12},{5,13},{6,14},{7,15},{8,0},{9,1},... | collective-permute-start | bytes 442376 | tf_op jit(solution)/shard_map/ppermute | solution.py:487
  65.4 4.7 %collective-permute-done.9.two.refs_8_ = f32[24,1536]{1,0:T(8,128)S(1)} collective-permute-done((f32[24,1536]{1,0:T(8,128)S(1)}, f32[24,1536]{1,0:T(8,128)S(1)}, u32[]{:S(2)}, u32[]{:S(2)}) %collective-permute-start.9) | collective-permute-done | bytes 147488 | tf_op jit(solution)/shard_map/ppermute | solution.py:487
  70.1 2.1 %shard_map.76 = (f32[2,6,2,16,128]{4,3,2,1,0:T(8,128)}, f32[2,6,2,16,128]{4,3,2,1,0:T(8,128)}, f32[2,6,2,16,128]{4,3,2,1,0:T(8,128)}, f32[2,6,2,16,128]{4,3,2,1,0:T(8,128)}) custom-call(f32[1]{0:T(128)} %div.15.refs_0_, f32[2,6,8,16,128]{4,3,2,1,0:T(8,128)} %bitcast.29, f32[2,6,8,16,128]{4,3,2,1,0:T(8,128)} %bitcast.6.refs_2_.up, ...), custom_call_target="tpu_custom_call" | custom-call | flops 1 | bytes 1 | tf_op jit(solution)/shard_map/pallas_call | solution.py:439
  72.2 2.0 %collective-permute-start.15 = (f32[12,2,16,128]{3,2,1,0:T(8,128)}, f32[12,2,16,128]{3,2,1,0:T(8,128)S(1)}, u32[]{:S(2)}, u32[]{:S(2)}) collective-permute-start(f32[12,2,16,128]{3,2,1,0:T(8,128)} %bitcast.43), channel_id=1, source_target_pairs={{0,48},{16,0},{32,16},{48,32},{1,49},{17,1},{33,17},{49,33},{2,50}... | collective-permute-start | bytes 589832 | tf_op jit(solution)/shard_map/ppermute | solution.py:349
  74.2 1.9 %collective-permute-start.17 = (f32[12,2,16,128]{3,2,1,0:T(8,128)}, f32[12,2,16,128]{3,2,1,0:T(8,128)S(1)}, u32[]{:S(2)}, u32[]{:S(2)}) collective-permute-start(f32[12,2,16,128]{3,2,1,0:T(8,128)} %bitcast.41), channel_id=1, source_target_pairs={{0,32},{16,48},{32,0},{48,16},{1,33},{17,49},{33,1},{49,17},{2,34}... | collective-permute-start | bytes 589832 | tf_op jit(solution)/shard_map/ppermute | solution.py:349
  77.2 5.0 %shard_map.77 = (f32[12,8,64,128]{3,2,1,0:T(8,128)}, f32[12,8,64,128]{3,2,1,0:T(8,128)}) custom-call(bf16[64,192]{1,0:T(8,128)(2,1)S(1)} %copy-done.6, f32[8,12,8,128]{3,2,1,0:T(8,128)S(1)} %shard_map.75.edge, f32[12,8,64,128]{3,2,1,0:T(8,128)S(1)} %bitcast.25, f32[12,6,64,128]{3,2,1,0:T(8,128)} %get-tuple-element.30.refs_5_.pre, ...), custom_call_target="tpu_custom_call" | custom-call | flops 1 | bytes 1 | tf_op jit(solution)/shard_map/pallas_call | solution.py:515
  82.2 4.2 %collective-permute-done.16.rest_2_ = f32[12,2,16,128]{3,2,1,0:T(8,128)S(1)} collective-permute-done((f32[12,2,16,128]{3,2,1,0:T(8,128)}, f32[12,2,16,128]{3,2,1,0:T(8,128)S(1)}, u32[]{:S(2)}, u32[]{:S(2)}) %collective-permute-start.16) | collective-permute-done | bytes 196640 | tf_op jit(solution)/shard_map/ppermute | solution.py:349
  86.4 2.3 %shard_map.78 = (f32[12,8,64,128]{3,2,1,0:T(8,128)}, f32[12,8,64,128]{3,2,1,0:T(8,128)}) custom-call(bf16[64,192]{1,0:T(8,128)(2,1)S(1)} %copy-done.6, f32[8,12,8,128]{3,2,1,0:T(8,128)S(1)} %shard_map.75.edge, f32[12,8,64,128]{3,2,1,0:T(8,128)S(1)} %bitcast.26, f32[12,2,64,128]{3,2,1,0:T(8,128)S(1)} %copy-done.4, ...), custom_call_target="tpu_custom_call", output_to_operand_aliasing={{0}: (8, {}), {1}: (9, {})} | custom-call | flops 1 | bytes 1 | tf_op jit(solution)/shard_map/pallas_call | solution.py:515
  (49 shorter events, 10.8 us)
Async XLA Ops:
  4.2 34.4 %collective-permute-start.3 = (f32[12,8,16,128]{3,2,1,0:T(8,128)}, f32[12,8,16,128]{3,2,1,0:T(8,128)}, u32[]{:S(2)}, u32[]{:S(2)}) collective-permute-start(f32[12,8,16,128]{3,2,1,0:T(8,128)} %get-tuple-element.26), channel_id=1, source_target_pairs={{0,48},{16,0},{32,16},{48,32},{1,49},{17,1},{33,17},{49,33},{2,50}... | collective-permute-start | bytes 2359304 | tf_op jit(solution)/shard_map/ppermute | solution.py:349
  6.8 31.8 %collective-permute-start.5 = (f32[12,8,16,128]{3,2,1,0:T(8,128)}, f32[12,8,16,128]{3,2,1,0:T(8,128)}, u32[]{:S(2)}, u32[]{:S(2)}) collective-permute-start(f32[12,8,16,128]{3,2,1,0:T(8,128)} %get-tuple-element.27), channel_id=1, source_target_pairs={{0,32},{16,48},{32,0},{48,16},{1,33},{17,49},{33,1},{49,17},{2,34}... | collective-permute-start | bytes 2359304 | tf_op jit(solution)/shard_map/ppermute | solution.py:349
  7.3 37.6 %collective-permute-start.4 = (f32[12,8,16,128]{3,2,1,0:T(8,128)}, f32[12,8,16,128]{3,2,1,0:T(8,128)}, u32[]{:S(2)}, u32[]{:S(2)}) collective-permute-start(f32[12,8,16,128]{3,2,1,0:T(8,128)} %get-tuple-element.24.after), channel_id=1, source_target_pairs={{0,16},{16,32},{32,48},{48,0},{1,17},{17,33},{33,49},{49,1},{2,18}... | collective-permute-start | bytes 2359304 | tf_op jit(solution)/shard_map/ppermute | solution.py:349
  9.5 23.4 %copy-start.1 = (f32[1,2,6,8,64,128]{5,4,3,2,1,0:T(8,128)S(1)}, f32[1,2,6,8,64,128]{5,4,3,2,1,0:T(8,128)}, u32[]{:S(2)}) copy-start(f32[1,2,6,8,64,128]{5,4,3,2,1,0:T(8,128)} %param.5) | copy-start | bytes 9437188
  9.6 23.4 %copy-start.3 = (f32[1,8,64,128]{3,2,1,0:T(8,128)S(1)}, f32[1,8,64,128]{3,2,1,0:T(8,128)}, u32[]{:S(2)}) copy-start(f32[1,8,64,128]{3,2,1,0:T(8,128)} %param.6) | copy-start | bytes 786436
  9.6 9.1 %collective-permute-start.1 = (f32[24,1536]{1,0:T(8,128)S(1)}, f32[24,1536]{1,0:T(8,128)S(1)}, u32[]{:S(2)}, u32[]{:S(2)}) collective-permute-start(f32[24,1536]{1,0:T(8,128)S(1)} %shard_map.69), channel_id=1, source_target_pairs={{0,65},{1,64},{2,67},{3,66},{4,69},{5,68},{6,71},{7,70},{8,73},{9,... | collective-permute-start | bytes 442376 | tf_op jit(solution)/shard_map/ppermute | solution.py:421
  13.9 7.5 %collective-permute-start = (f32[24,1536]{1,0:T(8,128)S(1)}, f32[24,1536]{1,0:T(8,128)S(1)}, u32[]{:S(2)}, u32[]{:S(2)}) collective-permute-start(f32[24,1536]{1,0:T(8,128)S(1)} %shard_map.69), channel_id=1, source_target_pairs={{0,64},{1,65},{2,66},{3,67},{4,68},{5,69},{6,70},{7,71},{8,72},{9,... | collective-permute-start | bytes 442376 | tf_op jit(solution)/shard_map/ppermute | solution.py:421
  18.7 6.6 %collective-permute-start.6 = (f32[12,64,128]{2,1,0:T(8,128)S(1)}, f32[12,64,128]{2,1,0:T(8,128)S(1)}, u32[]{:S(2)}, u32[]{:S(2)}) collective-permute-start(f32[12,64,128]{2,1,0:T(8,128)S(1)} %get-tuple-element.28), channel_id=1, source_target_pairs={{0,1},{1,2},{2,3},{3,4},{4,5},{5,6},{6,7},{7,8},{8,9},{9,10},{10,1... | collective-permute-start | bytes 1179656 | tf_op jit(solution)/shard_map/ppermute | solution.py:370
  21.5 11.5 %collective-permute-start.7 = (f32[12,64,128]{2,1,0:T(8,128)}, f32[12,64,128]{2,1,0:T(8,128)}, u32[]{:S(2)}, u32[]{:S(2)}) collective-permute-start(f32[12,64,128]{2,1,0:T(8,128)} %get-tuple-element.29), channel_id=1, source_target_pairs={{1,0},{2,1},{3,2},{4,3},{5,4},{6,5},{7,6},{8,7},{9,8},{10,9},{11,1... | collective-permute-start | bytes 1179656 | tf_op jit(solution)/shard_map/ppermute | solution.py:371
  26.1 12.5 %collective-permute-start.2 = (f32[24,1536]{1,0:T(8,128)}, f32[24,1536]{1,0:T(8,128)S(1)}, u32[]{:S(2)}, u32[]{:S(2)}) collective-permute-start(f32[24,1536]{1,0:T(8,128)} %add.26.one), channel_id=1, source_target_pairs={{0,2},{1,3},{2,0},{3,1},{4,6},{5,7},{6,4},{7,5},{8,10},{9,11},{10,... | collective-permute-start | bytes 442376 | tf_op jit(solution)/shard_map/ppermute | solution.py:423
  47.8 26.4 %collective-permute-start.10 = (f32[12,6,16,128]{3,2,1,0:T(8,128)}, f32[12,6,16,128]{3,2,1,0:T(8,128)}, u32[]{:S(2)}, u32[]{:S(2)}) collective-permute-start(f32[12,6,16,128]{3,2,1,0:T(8,128)} %bitcast.40), channel_id=1, source_target_pairs={{0,48},{16,0},{32,16},{48,32},{1,49},{17,1},{33,17},{49,33},{2,50}... | collective-permute-start | bytes 1769480 | tf_op jit(solution)/shard_map/ppermute | solution.py:349
  48.7 27.4 %collective-permute-start.11 = (f32[12,6,16,128]{3,2,1,0:T(8,128)}, f32[12,6,16,128]{3,2,1,0:T(8,128)S(1)}, u32[]{:S(2)}, u32[]{:S(2)}) collective-permute-start(f32[12,6,16,128]{3,2,1,0:T(8,128)} %bitcast.39), channel_id=1, source_target_pairs={{0,16},{16,32},{32,48},{48,0},{1,17},{17,33},{33,49},{49,1},{2,18}... | collective-permute-start | bytes 1769480 | tf_op jit(solution)/shard_map/ppermute | solution.py:349
  50.2 26.0 %collective-permute-start.12 = (f32[12,6,16,128]{3,2,1,0:T(8,128)}, f32[12,6,16,128]{3,2,1,0:T(8,128)S(1)}, u32[]{:S(2)}, u32[]{:S(2)}) collective-permute-start(f32[12,6,16,128]{3,2,1,0:T(8,128)} %bitcast.38), channel_id=1, source_target_pairs={{0,32},{16,48},{32,0},{48,16},{1,33},{17,49},{33,1},{49,17},{2,34}... | collective-permute-start | bytes 1769480 | tf_op jit(solution)/shard_map/ppermute | solution.py:349
  52.3 24.0 %copy-start.8 = (s32[8]{0:T(128)S(1)}, s32[8]{0:T(128)}, u32[]{:S(2)}) copy-start(s32[8]{0:T(128)} %orders.3) | copy-start | bytes 100
  53.2 5.6 %collective-permute-start.8 = (f32[24,1536]{1,0:T(8,128)S(1)}, f32[24,1536]{1,0:T(8,128)S(1)}, u32[]{:S(2)}, u32[]{:S(2)}) collective-permute-start(f32[24,1536]{1,0:T(8,128)S(1)} %shard_map.74), channel_id=1, source_target_pairs={{0,4},{1,5},{2,6},{3,7},{4,0},{5,1},{6,2},{7,3},{8,12},{9,13},{10,... | collective-permute-start | bytes 442376 | tf_op jit(solution)/shard_map/ppermute | solution.py:419
  53.6 5.9 %collective-permute-start.14 = (f32[4,6,16,128]{3,2,1,0:T(8,128)S(1)}, f32[4,6,16,128]{3,2,1,0:T(8,128)S(1)}, u32[]{:S(2)}, u32[]{:S(2)}) collective-permute-start(f32[4,6,16,128]{3,2,1,0:T(8,128)S(1)} %get-tuple-element.37), channel_id=1, source_target_pairs={{15,0},{0,15},{31,16},{16,31},{47,32},{32,47},{63,48},{48,63},{79,... | collective-permute-start | bytes 589832 | tf_op jit(solution)/shard_map/ppermute | solution.py:475
  58.8 6.6 %collective-permute-start.13 = (f32[4,6,16,128]{3,2,1,0:T(8,128)S(1)}, f32[4,6,16,128]{3,2,1,0:T(8,128)S(1)}, u32[]{:S(2)}, u32[]{:S(2)}) collective-permute-start(f32[4,6,16,128]{3,2,1,0:T(8,128)S(1)} %get-tuple-element.32.after), channel_id=1, source_target_pairs={{15,0},{0,15},{31,16},{16,31},{47,32},{32,47},{63,48},{48,63},{79,... | collective-permute-start | bytes 589832 | tf_op jit(solution)/shard_map/ppermute | solution.py:475
  59.5 17.6 %copy-start.6 = (bf16[64,192]{1,0:T(8,128)(2,1)S(1)}, bf16[64,192]{1,0:T(8,128)(2,1)}, u32[]{:S(2)}) copy-start(bf16[64,192]{1,0:T(8,128)(2,1)} %constant.38.clone.inverse) | copy-start | bytes 73732
  59.5 10.6 %collective-permute-start.9 = (f32[24,1536]{1,0:T(8,128)S(1)}, f32[24,1536]{1,0:T(8,128)S(1)}, u32[]{:S(2)}, u32[]{:S(2)}) collective-permute-start(f32[24,1536]{1,0:T(8,128)S(1)} %add.33.one), channel_id=1, source_target_pairs={{0,8},{1,9},{2,10},{3,11},{4,12},{5,13},{6,14},{7,15},{8,0},{9,1},... | collective-permute-start | bytes 442376 | tf_op jit(solution)/shard_map/ppermute | solution.py:487
  72.2 10.0 %collective-permute-start.15 = (f32[12,2,16,128]{3,2,1,0:T(8,128)}, f32[12,2,16,128]{3,2,1,0:T(8,128)S(1)}, u32[]{:S(2)}, u32[]{:S(2)}) collective-permute-start(f32[12,2,16,128]{3,2,1,0:T(8,128)} %bitcast.43), channel_id=1, source_target_pairs={{0,48},{16,0},{32,16},{48,32},{1,49},{17,1},{33,17},{49,33},{2,50}... | collective-permute-start | bytes 589832 | tf_op jit(solution)/shard_map/ppermute | solution.py:349
  74.2 12.2 %collective-permute-start.16 = (f32[12,2,16,128]{3,2,1,0:T(8,128)}, f32[12,2,16,128]{3,2,1,0:T(8,128)S(1)}, u32[]{:S(2)}, u32[]{:S(2)}) collective-permute-start(f32[12,2,16,128]{3,2,1,0:T(8,128)} %bitcast.42), channel_id=1, source_target_pairs={{0,16},{16,32},{32,48},{48,0},{1,17},{17,33},{33,49},{49,1},{2,18}... | collective-permute-start | bytes 589832 | tf_op jit(solution)/shard_map/ppermute | solution.py:349
  74.2 12.2 %collective-permute-start.17 = (f32[12,2,16,128]{3,2,1,0:T(8,128)}, f32[12,2,16,128]{3,2,1,0:T(8,128)S(1)}, u32[]{:S(2)}, u32[]{:S(2)}) collective-permute-start(f32[12,2,16,128]{3,2,1,0:T(8,128)} %bitcast.41), channel_id=1, source_target_pairs={{0,32},{16,48},{32,0},{48,16},{1,33},{17,49},{33,1},{49,17},{2,34}... | collective-permute-start | bytes 589832 | tf_op jit(solution)/shard_map/ppermute | solution.py:349
  77.1 9.3 %copy-start.4 = (f32[12,2,64,128]{3,2,1,0:T(8,128)S(1)}, f32[12,2,64,128]{3,2,1,0:T(8,128)}, u32[]{:S(2)}) copy-start(f32[12,2,64,128]{3,2,1,0:T(8,128)} %get-tuple-element.36.pre) | copy-start | bytes 2359300
  77.1 9.3 %copy-start.5 = (f32[2,6,2,16,128]{4,3,2,1,0:T(8,128)S(1)}, f32[2,6,2,16,128]{4,3,2,1,0:T(8,128)}, u32[]{:S(2)}) copy-start(f32[2,6,2,16,128]{4,3,2,1,0:T(8,128)} %get-tuple-element.38) | copy-start | bytes 589828
  (4 other events, 16.3 us)

commit v3 on v2

--- a/solution.py
+++ b/solution.py
@@ -134,9 +134,18 @@
         )
 
 
-def mix_kernel(scalars, own, up, down, far, after, *outs):
-    weight = [scalars[k] for k in range(INST)]
-    cosine, sine = scalars[INST], scalars[INST + 1]
+def mix_kernel(counts, own, up, down, far, after, *outs):
+    lanes = own.shape[-1]
+    which, low_end = lax.axis_index("row"), lax.axis_index("mesh") == 0
+    mine, other = (
+        jnp.full((1, lanes), counts[k], jnp.int32).astype(jnp.float32) for k in (which, 1 - which)
+    )
+    ratio, angle = other / mine, 2.0 * math.pi / mine
+    lag, turn = jnp.where(low_end, -ratio, ratio), jnp.where(low_end, angle, -angle)
+    delta = lax.broadcasted_iota(jnp.int32, (1, lanes), 1).astype(jnp.float32) - lag
+    weights = lag_weights(delta)
+    weight = [weights[:, k : k + 1] for k in range(INST)]
+    cosine, sine = jnp.cos(turn), jnp.sin(turn)
     at = jnp.where(lax.axis_index("mesh") == 0, 1, 0)
 
     def mixed(var):
@@ -320,8 +329,7 @@
         one.wait()
 
 
-def lag_weights(lag):
-    delta = jnp.arange(INST).astype(jnp.float32) - lag
+def lag_weights(delta):
     total = 1.0 + jnp.cos(math.pi * delta)
     for k in range(1, INST // 2):
         total = total + 2.0 * jnp.cos(2.0 * math.pi * k / INST * delta)
@@ -453,8 +461,6 @@
 
     one_source = sources(0, OUTER, (), after=(*in_hbm(pre_one), early))
 
-    weights = lag_weights(jnp.where(first, -ratio, ratio))
-    turn = jnp.where(first, angle, -angle)
     ghost_shape = shaped(INST // 2, variables, quarter, lanes)
 
     outermost = pl.BlockSpec((2, variables, 2, quarter, lanes), lambda b: (0, 0, 3, 0, 0))
@@ -467,7 +473,7 @@
         compiler_params=params(),
         cost_estimate=cost(),
     )(
-        jnp.concatenate([weights, jnp.stack([jnp.cos(turn), jnp.sin(turn)])]),
+        blade_counts,
         *all_quarters,
         *in_hbm(one_source[0]),
     )

time: 89.5 us -> 88.6 us (0.990)
  between operations: 3 us -> 2.08 us
  Pallas kernels: 30 us -> 30.9 us
  transfers between devices with their start and end apart: 18 -> 18, of which waited for: 9 -> 8; matrix products, arithmetic and copies ran while one was open for 4% -> 4% of each run, Pallas kernels for 24% -> 25%
where the time goes in v3:
time: 88.6 us; the launch traced here: 87.9 us
  Pallas kernels  30.9 us (35%)
  starting transfers between devices  27.5 us (31%)
  waiting for transfers between devices  22.3 us (25%)
  local copies, waits for them, and re-layouts  3.11 us (4%)
  between operations  2.08 us (2%)
  other arithmetic  1.93 us (2%)
    ppermute x9, waiting for transfers between devices, along(): return lax.ppermute(x, 'inst', [(j, (j + step) % 4) for j in range(4)])  9.96 us
    ppermute x9, starting transfers between devices, along(): return lax.ppermute(x, 'inst', [(j, (j + step) % 4) for j in range(4)])  9.57 us
    pallas_call x2, Pallas kernels, local(): pl.pallas_call(functools.partial(final_kernel, start, 4 if near else 2, n...  8.13 us
    ppermute x1, starting transfers between devices, local(): lax.ppermute(harmonics, 'mesh', [(m, m ^ 8) for m in range(mesh_count)])  5.85 us
    pallas_call x1, Pallas kernels, local(): pl.pallas_call(stencil_kernel, grid=(blocks // at_once,), out_shape=(pltp...  5.54 us
    pallas_call x2, Pallas kernels, sources(): pl.pallas_call(kernel, out_shape=(pltpu.HBM((*split, size, quarter, lanes...  5.02 us
    ppermute x1, waiting for transfers between devices, local(): lax.ppermute(harmonics, 'mesh', [(m, m ^ 8) for m in range(mesh_count)])  4.7 us
    ppermute x1, waiting for transfers between devices, doubled(): lax.ppermute(x, 'mesh', [(m, m ^ flip) for m in range(mesh_count)])  4.56 us
  transfers between devices with their start and end apart: 18, of which 8 were waited for; matrix products, arithmetic and copies ran while one was open for 4% of the time, Pallas kernels for 25%

profile of v3, /device:TPU:97, one launch (start us, length us, event | category | flops | bytes accessed | tf_op | source)
XLA Modules:
  0.0 87.9 jit_solution(15526937416855497701)
XLA Ops:
  0.7 3.6 %shard_map.68 = (f32[12,8,16,128]{3,2,1,0:T(8,128)}, f32[12,8,16,128]{3,2,1,0:T(8,128)}, f32[12,8,16,128]{3,2,1,0:T(8,128)}) custom-call(f32[12,8,64,128]{3,2,1,0:T(8,128)} %bitcast.16), custom_call_target="tpu_custom_call" | custom-call | flops 1 | bytes 1 | tf_op jit(solution)/shard_map/pallas_call | solution.py:103
  4.2 2.5 %collective-permute-start.3 = (f32[12,8,16,128]{3,2,1,0:T(8,128)}, f32[12,8,16,128]{3,2,1,0:T(8,128)}, u32[]{:S(2)}, u32[]{:S(2)}) collective-permute-start(f32[12,8,16,128]{3,2,1,0:T(8,128)} %get-tuple-element.26), channel_id=1, source_target_pairs={{0,48},{16,0},{32,16},{48,32},{1,49},{17,1},{33,17},{49,33},{2,50}... | collective-permute-start | bytes 2359304 | tf_op jit(solution)/shard_map/ppermute | solution.py:357
  7.9 1.6 %shard_map.69 = f32[24,1536]{1,0:T(8,128)S(1)} custom-call(s32[8]{0:T(128)S(1)} %copy-done.7, f32[12,8,16,128]{3,2,1,0:T(8,128)} %get-tuple-element.24.after, f32[12,8,64,128]{3,2,1,0:T(8,128)S(1)} %bitcast.18, f32[12,8,64,128]{3,2,1,0:T(8,128)S(1)} %bitcast.19), custom_call_target="tpu_custom_call" | custom-call | flops 1 | bytes 1 | tf_op jit(solution)/shard_map/pallas_call | solution.py:404
  9.6 4.4 %collective-permute-start.1 = (f32[24,1536]{1,0:T(8,128)S(1)}, f32[24,1536]{1,0:T(8,128)S(1)}, u32[]{:S(2)}, u32[]{:S(2)}) collective-permute-start(f32[24,1536]{1,0:T(8,128)S(1)} %shard_map.69), channel_id=1, source_target_pairs={{0,65},{1,64},{2,67},{3,66},{4,69},{5,68},{6,71},{7,70},{8,73},{9,... | collective-permute-start | bytes 442376 | tf_op jit(solution)/shard_map/ppermute | solution.py:429
  14.0 3.7 %shard_map.70 = (f32[12,64,128]{2,1,0:T(8,128)S(1)}, f32[12,64,128]{2,1,0:T(8,128)}, f32[12,8,16,128]{3,2,1,0:T(8,128)S(1)}) custom-call(f32[12,8,64,128]{3,2,1,0:T(8,128)} %bitcast.17, f32[12,8,16,128]{3,2,1,0:T(8,128)} %get-tuple-element.24.after), custom_call_target="tpu_custom_call" | custom-call | flops 1 | bytes 1 | tf_op jit(solution)/shard_map/pallas_call | solution.py:369
  18.7 1.9 %collective-permute-start.6 = (f32[12,64,128]{2,1,0:T(8,128)S(1)}, f32[12,64,128]{2,1,0:T(8,128)S(1)}, u32[]{:S(2)}, u32[]{:S(2)}) collective-permute-start(f32[12,64,128]{2,1,0:T(8,128)S(1)} %get-tuple-element.28), channel_id=1, source_target_pairs={{0,1},{1,2},{2,3},{3,4},{4,5},{5,6},{6,7},{7,8},{8,9},{9,10},{10,1... | collective-permute-start | bytes 1179656 | tf_op jit(solution)/shard_map/ppermute | solution.py:378
  21.5 2.4 %collective-permute-start.7 = (f32[12,64,128]{2,1,0:T(8,128)}, f32[12,64,128]{2,1,0:T(8,128)}, u32[]{:S(2)}, u32[]{:S(2)}) collective-permute-start(f32[12,64,128]{2,1,0:T(8,128)} %get-tuple-element.29), channel_id=1, source_target_pairs={{1,0},{2,1},{3,2},{4,3},{5,4},{6,5},{7,6},{8,7},{9,8},{10,9},{11,1... | collective-permute-start | bytes 1179656 | tf_op jit(solution)/shard_map/ppermute | solution.py:379
  26.1 1.7 %collective-permute-start.2 = (f32[24,1536]{1,0:T(8,128)}, f32[24,1536]{1,0:T(8,128)S(1)}, u32[]{:S(2)}, u32[]{:S(2)}) collective-permute-start(f32[24,1536]{1,0:T(8,128)} %add.13.one), channel_id=1, source_target_pairs={{0,2},{1,3},{2,0},{3,1},{4,6},{5,7},{6,4},{7,5},{8,10},{9,11},{10,... | collective-permute-start | bytes 442376 | tf_op jit(solution)/shard_map/ppermute | solution.py:431
  29.0 1.4 %fusion = (f32[1]{0:T(128)}, f32[1]{0:T(128)}) fusion(f32[2]{0:T(128)} %convert_element_type.3, s32[]{:T(128)S(6)} %select_n.7, s32[]{:T(128)S(6)} %select_n.6), kind=kLoop, calls=%fused_computation | loop fusion | bytes 24 | tf_op jit(solution)/shard_map/dynamic_slice | solution.py:349
  31.6 1.4 %collective-permute-done.7.high = f32[12,64,128]{2,1,0:T(8,128)} collective-permute-done((f32[12,64,128]{2,1,0:T(8,128)}, f32[12,64,128]{2,1,0:T(8,128)}, u32[]{:S(2)}, u32[]{:S(2)}) %collective-permute-start.7) | collective-permute-done | bytes 393248 | tf_op jit(solution)/shard_map/ppermute | solution.py:379
  33.0 5.5 %shard_map.71 = (f32[12,6,64,128]{3,2,1,0:T(8,128)}, f32[12,2,64,128]{3,2,1,0:T(8,128)}) custom-call(f32[8,64,128]{2,1,0:T(8,128)S(1)} %bitcast.26, f32[12,64,128]{2,1,0:T(8,128)} %copy-done.10, f32[12,64,128]{2,1,0:T(8,128)} %collective-permute-done.7.high, f32[12,8,64,128]{3,2,1,0:T(8,128)S(1)} %bitcast.20), custom_call_target="tpu_custom_call" | custom-call | flops 1 | bytes 1 | tf_op jit(solution)/shard_map/pallas_call | solution.py:388
  38.6 6.3 %collective-permute-done.4 = f32[12,8,16,128]{3,2,1,0:T(8,128)} collective-permute-done((f32[12,8,16,128]{3,2,1,0:T(8,128)}, f32[12,8,16,128]{3,2,1,0:T(8,128)}, u32[]{:S(2)}, u32[]{:S(2)}) %collective-permute-start.4) | collective-permute-done | bytes 786464 | tf_op jit(solution)/shard_map/ppermute | solution.py:357
  44.9 2.9 %shard_map.72 = (f32[2,6,6,16,128]{4,3,2,1,0:T(8,128)}, f32[2,6,6,16,128]{4,3,2,1,0:T(8,128)}, f32[2,6,6,16,128]{4,3,2,1,0:T(8,128)}, f32[2,6,6,16,128]{4,3,2,1,0:T(8,128)}) custom-call(f32[1]{0:T(128)S(6)} %div.4.refs_0_, f32[2,6,8,16,128]{4,3,2,1,0:T(8,128)} %bitcast.23, f32[2,6,8,16,128]{4,3,2,1,0:T(8,128)} %bitcast.2.refs_2_.up, ...), custom_call_target="tpu_custom_call" | custom-call | flops 1 | bytes 1 | tf_op jit(solution)/shard_map/pallas_call | solution.py:447
  47.8 1.5 %collective-permute-start.11 = (f32[12,6,16,128]{3,2,1,0:T(8,128)}, f32[12,6,16,128]{3,2,1,0:T(8,128)S(1)}, u32[]{:S(2)}, u32[]{:S(2)}) collective-permute-start(f32[12,6,16,128]{3,2,1,0:T(8,128)} %bitcast.35), channel_id=1, source_target_pairs={{0,16},{16,32},{32,48},{48,0},{1,17},{17,33},{33,49},{49,1},{2,18}... | collective-permute-start | bytes 1769480 | tf_op jit(solution)/shard_map/ppermute | solution.py:357
  49.8 1.6 %shard_map.73 = (f32[4,6,16,128]{3,2,1,0:T(8,128)S(1)}, f32[4,6,16,128]{3,2,1,0:T(8,128)S(1)}) custom-call(s32[2]{0:T(128)S(1)} %copy-done.9, f32[2,6,8,16,128]{4,3,2,1,0:T(8,128)} %bitcast.24, f32[2,6,8,16,128]{4,3,2,1,0:T(8,128)} %bitcast.2.refs_2_.up, f32[2,6,8,16,128]{4,3,2,1,0:T(8,128)} %bitcast.3.refs_3_.down, ...), custom_call_target="tpu_custom_call" | custom-call | flops 1 | bytes 1 | tf_op jit(solution)/shard_map/pallas_call | solution.py:467
  53.4 4.6 %collective-permute-done.8 = f32[24,1536]{1,0:T(8,128)S(1)} collective-permute-done((f32[24,1536]{1,0:T(8,128)S(1)}, f32[24,1536]{1,0:T(8,128)S(1)}, u32[]{:S(2)}, u32[]{:S(2)}) %collective-permute-start.8) | collective-permute-done | bytes 147488 | tf_op jit(solution)/shard_map/ppermute | solution.py:427
  58.6 5.9 %collective-permute-start.9 = (f32[24,1536]{1,0:T(8,128)S(1)}, f32[24,1536]{1,0:T(8,128)S(1)}, u32[]{:S(2)}, u32[]{:S(2)}) collective-permute-start(f32[24,1536]{1,0:T(8,128)S(1)} %add.16.one), channel_id=1, source_target_pairs={{0,8},{1,9},{2,10},{3,11},{4,12},{5,13},{6,14},{7,15},{8,0},{9,1},... | collective-permute-start | bytes 442376 | tf_op jit(solution)/shard_map/ppermute | solution.py:493
  64.5 4.7 %collective-permute-done.9.two.refs_8_ = f32[24,1536]{1,0:T(8,128)S(1)} collective-permute-done((f32[24,1536]{1,0:T(8,128)S(1)}, f32[24,1536]{1,0:T(8,128)S(1)}, u32[]{:S(2)}, u32[]{:S(2)}) %collective-permute-start.9) | collective-permute-done | bytes 147488 | tf_op jit(solution)/shard_map/ppermute | solution.py:493
  69.2 2.1 %shard_map.76 = (f32[2,6,2,16,128]{4,3,2,1,0:T(8,128)}, f32[2,6,2,16,128]{4,3,2,1,0:T(8,128)}, f32[2,6,2,16,128]{4,3,2,1,0:T(8,128)}, f32[2,6,2,16,128]{4,3,2,1,0:T(8,128)}) custom-call(f32[1]{0:T(128)S(6)} %div.4.refs_0_, f32[2,6,8,16,128]{4,3,2,1,0:T(8,128)} %bitcast.25, f32[2,6,8,16,128]{4,3,2,1,0:T(8,128)} %bitcast.2.refs_2_.up, ...), custom_call_target="tpu_custom_call" | custom-call | flops 1 | bytes 1 | tf_op jit(solution)/shard_map/pallas_call | solution.py:447
  71.3 1.9 %collective-permute-start.15 = (f32[12,2,16,128]{3,2,1,0:T(8,128)}, f32[12,2,16,128]{3,2,1,0:T(8,128)S(1)}, u32[]{:S(2)}, u32[]{:S(2)}) collective-permute-start(f32[12,2,16,128]{3,2,1,0:T(8,128)} %bitcast.39), channel_id=1, source_target_pairs={{0,48},{16,0},{32,16},{48,32},{1,49},{17,1},{33,17},{49,33},{2,50}... | collective-permute-start | bytes 589832 | tf_op jit(solution)/shard_map/ppermute | solution.py:357
  73.2 2.0 %collective-permute-start.17 = (f32[12,2,16,128]{3,2,1,0:T(8,128)}, f32[12,2,16,128]{3,2,1,0:T(8,128)S(1)}, u32[]{:S(2)}, u32[]{:S(2)}) collective-permute-start(f32[12,2,16,128]{3,2,1,0:T(8,128)} %bitcast.37), channel_id=1, source_target_pairs={{0,32},{16,48},{32,0},{48,16},{1,33},{17,49},{33,1},{49,17},{2,34}... | collective-permute-start | bytes 589832 | tf_op jit(solution)/shard_map/ppermute | solution.py:357
  76.2 5.8 %shard_map.77 = (f32[12,8,64,128]{3,2,1,0:T(8,128)}, f32[12,8,64,128]{3,2,1,0:T(8,128)}) custom-call(bf16[64,192]{1,0:T(8,128)(2,1)S(1)} %copy-done.6, f32[8,12,8,128]{3,2,1,0:T(8,128)S(1)} %shard_map.75.edge, f32[12,8,64,128]{3,2,1,0:T(8,128)S(1)} %bitcast.21, f32[12,6,64,128]{3,2,1,0:T(8,128)} %get-tuple-element.30.refs_5_.pre, ...), custom_call_target="tpu_custom_call" | custom-call | flops 1 | bytes 1 | tf_op jit(solution)/shard_map/pallas_call | solution.py:521
  82.0 3.6 %collective-permute-done.16.rest_2_ = f32[12,2,16,128]{3,2,1,0:T(8,128)S(1)} collective-permute-done((f32[12,2,16,128]{3,2,1,0:T(8,128)}, f32[12,2,16,128]{3,2,1,0:T(8,128)S(1)}, u32[]{:S(2)}, u32[]{:S(2)}) %collective-permute-start.16) | collective-permute-done | bytes 196640 | tf_op jit(solution)/shard_map/ppermute | solution.py:357
  85.6 2.3 %shard_map.78 = (f32[12,8,64,128]{3,2,1,0:T(8,128)}, f32[12,8,64,128]{3,2,1,0:T(8,128)}) custom-call(bf16[64,192]{1,0:T(8,128)(2,1)S(1)} %copy-done.6, f32[8,12,8,128]{3,2,1,0:T(8,128)S(1)} %shard_map.75.edge, f32[12,8,64,128]{3,2,1,0:T(8,128)S(1)} %bitcast.22, f32[12,2,64,128]{3,2,1,0:T(8,128)S(1)} %copy-done.4, ...), custom_call_target="tpu_custom_call", output_to_operand_aliasing={{0}: (8, {}), {1}: (9, {})} | custom-call | flops 1 | bytes 1 | tf_op jit(solution)/shard_map/pallas_call | solution.py:521
  (49 shorter events, 10.6 us)
Async XLA Ops:
  4.2 34.3 %collective-permute-start.3 = (f32[12,8,16,128]{3,2,1,0:T(8,128)}, f32[12,8,16,128]{3,2,1,0:T(8,128)}, u32[]{:S(2)}, u32[]{:S(2)}) collective-permute-start(f32[12,8,16,128]{3,2,1,0:T(8,128)} %get-tuple-element.26), channel_id=1, source_target_pairs={{0,48},{16,0},{32,16},{48,32},{1,49},{17,1},{33,17},{49,33},{2,50}... | collective-permute-start | bytes 2359304 | tf_op jit(solution)/shard_map/ppermute | solution.py:357
  6.8 31.8 %collective-permute-start.5 = (f32[12,8,16,128]{3,2,1,0:T(8,128)}, f32[12,8,16,128]{3,2,1,0:T(8,128)}, u32[]{:S(2)}, u32[]{:S(2)}) collective-permute-start(f32[12,8,16,128]{3,2,1,0:T(8,128)} %get-tuple-element.27), channel_id=1, source_target_pairs={{0,32},{16,48},{32,0},{48,16},{1,33},{17,49},{33,1},{49,17},{2,34}... | collective-permute-start | bytes 2359304 | tf_op jit(solution)/shard_map/ppermute | solution.py:357
  7.3 37.6 %collective-permute-start.4 = (f32[12,8,16,128]{3,2,1,0:T(8,128)}, f32[12,8,16,128]{3,2,1,0:T(8,128)}, u32[]{:S(2)}, u32[]{:S(2)}) collective-permute-start(f32[12,8,16,128]{3,2,1,0:T(8,128)} %get-tuple-element.24.after), channel_id=1, source_target_pairs={{0,16},{16,32},{32,48},{48,0},{1,17},{17,33},{33,49},{49,1},{2,18}... | collective-permute-start | bytes 2359304 | tf_op jit(solution)/shard_map/ppermute | solution.py:357
  9.6 23.4 %copy-start.1 = (f32[1,2,6,8,64,128]{5,4,3,2,1,0:T(8,128)S(1)}, f32[1,2,6,8,64,128]{5,4,3,2,1,0:T(8,128)}, u32[]{:S(2)}) copy-start(f32[1,2,6,8,64,128]{5,4,3,2,1,0:T(8,128)} %param.5) | copy-start | bytes 9437188
  9.6 23.4 %copy-start.3 = (f32[1,8,64,128]{3,2,1,0:T(8,128)S(1)}, f32[1,8,64,128]{3,2,1,0:T(8,128)}, u32[]{:S(2)}) copy-start(f32[1,8,64,128]{3,2,1,0:T(8,128)} %param.6) | copy-start | bytes 786436
  9.6 9.1 %collective-permute-start.1 = (f32[24,1536]{1,0:T(8,128)S(1)}, f32[24,1536]{1,0:T(8,128)S(1)}, u32[]{:S(2)}, u32[]{:S(2)}) collective-permute-start(f32[24,1536]{1,0:T(8,128)S(1)} %shard_map.69), channel_id=1, source_target_pairs={{0,65},{1,64},{2,67},{3,66},{4,69},{5,68},{6,71},{7,70},{8,73},{9,... | collective-permute-start | bytes 442376 | tf_op jit(solution)/shard_map/ppermute | solution.py:429
  13.9 7.5 %collective-permute-start = (f32[24,1536]{1,0:T(8,128)S(1)}, f32[24,1536]{1,0:T(8,128)S(1)}, u32[]{:S(2)}, u32[]{:S(2)}) collective-permute-start(f32[24,1536]{1,0:T(8,128)S(1)} %shard_map.69), channel_id=1, source_target_pairs={{0,64},{1,65},{2,66},{3,67},{4,68},{5,69},{6,70},{7,71},{8,72},{9,... | collective-permute-start | bytes 442376 | tf_op jit(solution)/shard_map/ppermute | solution.py:429
  18.7 6.6 %collective-permute-start.6 = (f32[12,64,128]{2,1,0:T(8,128)S(1)}, f32[12,64,128]{2,1,0:T(8,128)S(1)}, u32[]{:S(2)}, u32[]{:S(2)}) collective-permute-start(f32[12,64,128]{2,1,0:T(8,128)S(1)} %get-tuple-element.28), channel_id=1, source_target_pairs={{0,1},{1,2},{2,3},{3,4},{4,5},{5,6},{6,7},{7,8},{8,9},{9,10},{10,1... | collective-permute-start | bytes 1179656 | tf_op jit(solution)/shard_map/ppermute | solution.py:378
  21.5 11.5 %collective-permute-start.7 = (f32[12,64,128]{2,1,0:T(8,128)}, f32[12,64,128]{2,1,0:T(8,128)}, u32[]{:S(2)}, u32[]{:S(2)}) collective-permute-start(f32[12,64,128]{2,1,0:T(8,128)} %get-tuple-element.29), channel_id=1, source_target_pairs={{1,0},{2,1},{3,2},{4,3},{5,4},{6,5},{7,6},{8,7},{9,8},{10,9},{11,1... | collective-permute-start | bytes 1179656 | tf_op jit(solution)/shard_map/ppermute | solution.py:379
  26.1 12.5 %collective-permute-start.2 = (f32[24,1536]{1,0:T(8,128)}, f32[24,1536]{1,0:T(8,128)S(1)}, u32[]{:S(2)}, u32[]{:S(2)}) collective-permute-start(f32[24,1536]{1,0:T(8,128)} %add.13.one), channel_id=1, source_target_pairs={{0,2},{1,3},{2,0},{3,1},{4,6},{5,7},{6,4},{7,5},{8,10},{9,11},{10,... | collective-permute-start | bytes 442376 | tf_op jit(solution)/shard_map/ppermute | solution.py:431
  38.5 11.2 %copy-start.9 = (s32[2]{0:T(128)S(1)}, s32[2]{0:T(128)}, u32[]{:S(2)}) copy-start(s32[2]{0:T(128)} %counts.1) | copy-start | bytes 28
  47.8 25.4 %collective-permute-start.10 = (f32[12,6,16,128]{3,2,1,0:T(8,128)}, f32[12,6,16,128]{3,2,1,0:T(8,128)S(1)}, u32[]{:S(2)}, u32[]{:S(2)}) collective-permute-start(f32[12,6,16,128]{3,2,1,0:T(8,128)} %bitcast.36), channel_id=1, source_target_pairs={{0,48},{16,0},{32,16},{48,32},{1,49},{17,1},{33,17},{49,33},{2,50}... | collective-permute-start | bytes 1769480 | tf_op jit(solution)/shard_map/ppermute | solution.py:357
  47.8 27.5 %collective-permute-start.11 = (f32[12,6,16,128]{3,2,1,0:T(8,128)}, f32[12,6,16,128]{3,2,1,0:T(8,128)S(1)}, u32[]{:S(2)}, u32[]{:S(2)}) collective-permute-start(f32[12,6,16,128]{3,2,1,0:T(8,128)} %bitcast.35), channel_id=1, source_target_pairs={{0,16},{16,32},{32,48},{48,0},{1,17},{17,33},{33,49},{49,1},{2,18}... | collective-permute-start | bytes 1769480 | tf_op jit(solution)/shard_map/ppermute | solution.py:357
  49.3 26.0 %collective-permute-start.12 = (f32[12,6,16,128]{3,2,1,0:T(8,128)}, f32[12,6,16,128]{3,2,1,0:T(8,128)S(1)}, u32[]{:S(2)}, u32[]{:S(2)}) collective-permute-start(f32[12,6,16,128]{3,2,1,0:T(8,128)} %bitcast.34), channel_id=1, source_target_pairs={{0,32},{16,48},{32,0},{48,16},{1,33},{17,49},{33,1},{49,17},{2,34}... | collective-permute-start | bytes 1769480 | tf_op jit(solution)/shard_map/ppermute | solution.py:357
  51.4 23.9 %copy-start.8 = (s32[8]{0:T(128)S(1)}, s32[8]{0:T(128)}, u32[]{:S(2)}) copy-start(s32[8]{0:T(128)} %orders.3) | copy-start | bytes 100
  52.3 5.6 %collective-permute-start.8 = (f32[24,1536]{1,0:T(8,128)S(1)}, f32[24,1536]{1,0:T(8,128)S(1)}, u32[]{:S(2)}, u32[]{:S(2)}) collective-permute-start(f32[24,1536]{1,0:T(8,128)S(1)} %shard_map.74), channel_id=1, source_target_pairs={{0,4},{1,5},{2,6},{3,7},{4,0},{5,1},{6,2},{7,3},{8,12},{9,13},{10,... | collective-permute-start | bytes 442376 | tf_op jit(solution)/shard_map/ppermute | solution.py:427
  52.7 5.9 %collective-permute-start.14 = (f32[4,6,16,128]{3,2,1,0:T(8,128)S(1)}, f32[4,6,16,128]{3,2,1,0:T(8,128)S(1)}, u32[]{:S(2)}, u32[]{:S(2)}) collective-permute-start(f32[4,6,16,128]{3,2,1,0:T(8,128)S(1)} %get-tuple-element.37), channel_id=1, source_target_pairs={{15,0},{0,15},{31,16},{16,31},{47,32},{32,47},{63,48},{48,63},{79,... | collective-permute-start | bytes 589832 | tf_op jit(solution)/shard_map/ppermute | solution.py:481
  57.9 6.6 %collective-permute-start.13 = (f32[4,6,16,128]{3,2,1,0:T(8,128)S(1)}, f32[4,6,16,128]{3,2,1,0:T(8,128)S(1)}, u32[]{:S(2)}, u32[]{:S(2)}) collective-permute-start(f32[4,6,16,128]{3,2,1,0:T(8,128)S(1)} %get-tuple-element.32.after), channel_id=1, source_target_pairs={{15,0},{0,15},{31,16},{16,31},{47,32},{32,47},{63,48},{48,63},{79,... | collective-permute-start | bytes 589832 | tf_op jit(solution)/shard_map/ppermute | solution.py:481
  58.6 17.5 %copy-start.6 = (bf16[64,192]{1,0:T(8,128)(2,1)S(1)}, bf16[64,192]{1,0:T(8,128)(2,1)}, u32[]{:S(2)}) copy-start(bf16[64,192]{1,0:T(8,128)(2,1)} %constant.16.clone.inverse) | copy-start | bytes 73732
  58.6 10.6 %collective-permute-start.9 = (f32[24,1536]{1,0:T(8,128)S(1)}, f32[24,1536]{1,0:T(8,128)S(1)}, u32[]{:S(2)}, u32[]{:S(2)}) collective-permute-start(f32[24,1536]{1,0:T(8,128)S(1)} %add.16.one), channel_id=1, source_target_pairs={{0,8},{1,9},{2,10},{3,11},{4,12},{5,13},{6,14},{7,15},{8,0},{9,1},... | collective-permute-start | bytes 442376 | tf_op jit(solution)/shard_map/ppermute | solution.py:493
  71.3 10.6 %collective-permute-start.15 = (f32[12,2,16,128]{3,2,1,0:T(8,128)}, f32[12,2,16,128]{3,2,1,0:T(8,128)S(1)}, u32[]{:S(2)}, u32[]{:S(2)}) collective-permute-start(f32[12,2,16,128]{3,2,1,0:T(8,128)} %bitcast.39), channel_id=1, source_target_pairs={{0,48},{16,0},{32,16},{48,32},{1,49},{17,1},{33,17},{49,33},{2,50}... | collective-permute-start | bytes 589832 | tf_op jit(solution)/shard_map/ppermute | solution.py:357
  73.2 12.3 %collective-permute-start.16 = (f32[12,2,16,128]{3,2,1,0:T(8,128)}, f32[12,2,16,128]{3,2,1,0:T(8,128)S(1)}, u32[]{:S(2)}, u32[]{:S(2)}) collective-permute-start(f32[12,2,16,128]{3,2,1,0:T(8,128)} %bitcast.38), channel_id=1, source_target_pairs={{0,16},{16,32},{32,48},{48,0},{1,17},{17,33},{33,49},{49,1},{2,18}... | collective-permute-start | bytes 589832 | tf_op jit(solution)/shard_map/ppermute | solution.py:357
  73.2 12.3 %collective-permute-start.17 = (f32[12,2,16,128]{3,2,1,0:T(8,128)}, f32[12,2,16,128]{3,2,1,0:T(8,128)S(1)}, u32[]{:S(2)}, u32[]{:S(2)}) collective-permute-start(f32[12,2,16,128]{3,2,1,0:T(8,128)} %bitcast.37), channel_id=1, source_target_pairs={{0,32},{16,48},{32,0},{48,16},{1,33},{17,49},{33,1},{49,17},{2,34}... | collective-permute-start | bytes 589832 | tf_op jit(solution)/shard_map/ppermute | solution.py:357
  76.1 9.4 %copy-start.4 = (f32[12,2,64,128]{3,2,1,0:T(8,128)S(1)}, f32[12,2,64,128]{3,2,1,0:T(8,128)}, u32[]{:S(2)}) copy-start(f32[12,2,64,128]{3,2,1,0:T(8,128)} %get-tuple-element.36.pre) | copy-start | bytes 2359300
  (5 other events, 25.7 us)

commit v4 on v3

--- a/solution.py
+++ b/solution.py
@@ -519,7 +519,7 @@
         else:
             given_in = (*in_hbm(pre, group[0]), *group[1:])
         kept = pl.pallas_call(
-            functools.partial(final_kernel, start, 4 if near else 2, near),
+            functools.partial(final_kernel, start, 2, near),
             out_shape=(pltpu.HBM(field.shape, jnp.float32),) * 2,
             in_specs=[VMEM] * 3
             + ([VMEM] * 5 if near else [HBM] * 2 + [ANY] * 3)

time: 88.6 us -> 88.7 us (level)
  no operation moved by 1% of the time
where the time goes in v4:
time: 88.7 us; the launch traced here: 88 us
  Pallas kernels  31 us (35%)
  starting transfers between devices  27.5 us (31%)
  waiting for transfers between devices  22.3 us (25%)
  local copies, waits for them, and re-layouts  3.11 us (4%)
  between operations  2.08 us (2%)
  other arithmetic  1.93 us (2%)
    ppermute x9, waiting for transfers between devices, along(): return lax.ppermute(x, 'inst', [(j, (j + step) % 4) for j in range(4)])  9.96 us
    ppermute x9, starting transfers between devices, along(): return lax.ppermute(x, 'inst', [(j, (j + step) % 4) for j in range(4)])  9.57 us
    pallas_call x2, Pallas kernels, local(): pl.pallas_call(functools.partial(final_kernel, start, 2, near), out_shape...  8.2 us
    ppermute x1, starting transfers between devices, local(): lax.ppermute(harmonics, 'mesh', [(m, m ^ 8) for m in range(mesh_count)])  5.85 us
    pallas_call x1, Pallas kernels, local(): pl.pallas_call(stencil_kernel, grid=(blocks // at_once,), out_shape=(pltp...  5.54 us
    pallas_call x2, Pallas kernels, sources(): pl.pallas_call(kernel, out_shape=(pltpu.HBM((*split, size, quarter, lanes...  5.02 us
    ppermute x1, waiting for transfers between devices, local(): lax.ppermute(harmonics, 'mesh', [(m, m ^ 8) for m in range(mesh_count)])  4.7 us
    ppermute x1, waiting for transfers between devices, doubled(): lax.ppermute(x, 'mesh', [(m, m ^ flip) for m in range(mesh_count)])  4.56 us
  transfers between devices with their start and end apart: 18, of which 8 were waited for; matrix products, arithmetic and copies ran while one was open for 4% of the time, Pallas kernels for 25%

profile of v4, /device:TPU:97, one launch (start us, length us, event | category | flops | bytes accessed | tf_op | source)
XLA Modules:
  0.0 88.0 jit_solution(8256695857334669602)
XLA Ops:
  0.7 3.6 %shard_map.68 = (f32[12,8,16,128]{3,2,1,0:T(8,128)}, f32[12,8,16,128]{3,2,1,0:T(8,128)}, f32[12,8,16,128]{3,2,1,0:T(8,128)}) custom-call(f32[12,8,64,128]{3,2,1,0:T(8,128)} %bitcast.16), custom_call_target="tpu_custom_call" | custom-call | flops 1 | bytes 1 | tf_op jit(solution)/shard_map/pallas_call | solution.py:103
  4.2 2.5 %collective-permute-start.3 = (f32[12,8,16,128]{3,2,1,0:T(8,128)}, f32[12,8,16,128]{3,2,1,0:T(8,128)}, u32[]{:S(2)}, u32[]{:S(2)}) collective-permute-start(f32[12,8,16,128]{3,2,1,0:T(8,128)} %get-tuple-element.26), channel_id=1, source_target_pairs={{0,48},{16,0},{32,16},{48,32},{1,49},{17,1},{33,17},{49,33},{2,50}... | collective-permute-start | bytes 2359304 | tf_op jit(solution)/shard_map/ppermute | solution.py:357
  7.9 1.6 %shard_map.69 = f32[24,1536]{1,0:T(8,128)S(1)} custom-call(s32[8]{0:T(128)S(1)} %copy-done.7, f32[12,8,16,128]{3,2,1,0:T(8,128)} %get-tuple-element.24.after, f32[12,8,64,128]{3,2,1,0:T(8,128)S(1)} %bitcast.18, f32[12,8,64,128]{3,2,1,0:T(8,128)S(1)} %bitcast.19), custom_call_target="tpu_custom_call" | custom-call | flops 1 | bytes 1 | tf_op jit(solution)/shard_map/pallas_call | solution.py:404
  9.6 4.4 %collective-permute-start.1 = (f32[24,1536]{1,0:T(8,128)S(1)}, f32[24,1536]{1,0:T(8,128)S(1)}, u32[]{:S(2)}, u32[]{:S(2)}) collective-permute-start(f32[24,1536]{1,0:T(8,128)S(1)} %shard_map.69), channel_id=1, source_target_pairs={{0,65},{1,64},{2,67},{3,66},{4,69},{5,68},{6,71},{7,70},{8,73},{9,... | collective-permute-start | bytes 442376 | tf_op jit(solution)/shard_map/ppermute | solution.py:429
  14.0 3.7 %shard_map.70 = (f32[12,64,128]{2,1,0:T(8,128)S(1)}, f32[12,64,128]{2,1,0:T(8,128)}, f32[12,8,16,128]{3,2,1,0:T(8,128)S(1)}) custom-call(f32[12,8,64,128]{3,2,1,0:T(8,128)} %bitcast.17, f32[12,8,16,128]{3,2,1,0:T(8,128)} %get-tuple-element.24.after), custom_call_target="tpu_custom_call" | custom-call | flops 1 | bytes 1 | tf_op jit(solution)/shard_map/pallas_call | solution.py:369
  18.7 1.9 %collective-permute-start.6 = (f32[12,64,128]{2,1,0:T(8,128)S(1)}, f32[12,64,128]{2,1,0:T(8,128)S(1)}, u32[]{:S(2)}, u32[]{:S(2)}) collective-permute-start(f32[12,64,128]{2,1,0:T(8,128)S(1)} %get-tuple-element.28), channel_id=1, source_target_pairs={{0,1},{1,2},{2,3},{3,4},{4,5},{5,6},{6,7},{7,8},{8,9},{9,10},{10,1... | collective-permute-start | bytes 1179656 | tf_op jit(solution)/shard_map/ppermute | solution.py:378
  21.5 2.4 %collective-permute-start.7 = (f32[12,64,128]{2,1,0:T(8,128)}, f32[12,64,128]{2,1,0:T(8,128)}, u32[]{:S(2)}, u32[]{:S(2)}) collective-permute-start(f32[12,64,128]{2,1,0:T(8,128)} %get-tuple-element.29), channel_id=1, source_target_pairs={{1,0},{2,1},{3,2},{4,3},{5,4},{6,5},{7,6},{8,7},{9,8},{10,9},{11,1... | collective-permute-start | bytes 1179656 | tf_op jit(solution)/shard_map/ppermute | solution.py:379
  26.1 1.7 %collective-permute-start.2 = (f32[24,1536]{1,0:T(8,128)}, f32[24,1536]{1,0:T(8,128)S(1)}, u32[]{:S(2)}, u32[]{:S(2)}) collective-permute-start(f32[24,1536]{1,0:T(8,128)} %add.13.one), channel_id=1, source_target_pairs={{0,2},{1,3},{2,0},{3,1},{4,6},{5,7},{6,4},{7,5},{8,10},{9,11},{10,... | collective-permute-start | bytes 442376 | tf_op jit(solution)/shard_map/ppermute | solution.py:431
  29.0 1.4 %fusion = (f32[1]{0:T(128)}, f32[1]{0:T(128)}) fusion(f32[2]{0:T(128)} %convert_element_type.3, s32[]{:T(128)S(6)} %select_n.7, s32[]{:T(128)S(6)} %select_n.6), kind=kLoop, calls=%fused_computation | loop fusion | bytes 24 | tf_op jit(solution)/shard_map/dynamic_slice | solution.py:349
  31.6 1.4 %collective-permute-done.7.high = f32[12,64,128]{2,1,0:T(8,128)} collective-permute-done((f32[12,64,128]{2,1,0:T(8,128)}, f32[12,64,128]{2,1,0:T(8,128)}, u32[]{:S(2)}, u32[]{:S(2)}) %collective-permute-start.7) | collective-permute-done | bytes 393248 | tf_op jit(solution)/shard_map/ppermute | solution.py:379
  33.0 5.5 %shard_map.71 = (f32[12,6,64,128]{3,2,1,0:T(8,128)}, f32[12,2,64,128]{3,2,1,0:T(8,128)}) custom-call(f32[8,64,128]{2,1,0:T(8,128)S(1)} %bitcast.26, f32[12,64,128]{2,1,0:T(8,128)} %copy-done.10, f32[12,64,128]{2,1,0:T(8,128)} %collective-permute-done.7.high, f32[12,8,64,128]{3,2,1,0:T(8,128)S(1)} %bitcast.20), custom_call_target="tpu_custom_call" | custom-call | flops 1 | bytes 1 | tf_op jit(solution)/shard_map/pallas_call | solution.py:388
  38.6 6.3 %collective-permute-done.4 = f32[12,8,16,128]{3,2,1,0:T(8,128)} collective-permute-done((f32[12,8,16,128]{3,2,1,0:T(8,128)}, f32[12,8,16,128]{3,2,1,0:T(8,128)}, u32[]{:S(2)}, u32[]{:S(2)}) %collective-permute-start.4) | collective-permute-done | bytes 786464 | tf_op jit(solution)/shard_map/ppermute | solution.py:357
  44.9 2.9 %shard_map.72 = (f32[2,6,6,16,128]{4,3,2,1,0:T(8,128)}, f32[2,6,6,16,128]{4,3,2,1,0:T(8,128)}, f32[2,6,6,16,128]{4,3,2,1,0:T(8,128)}, f32[2,6,6,16,128]{4,3,2,1,0:T(8,128)}) custom-call(f32[1]{0:T(128)S(6)} %div.4.refs_0_, f32[2,6,8,16,128]{4,3,2,1,0:T(8,128)} %bitcast.23, f32[2,6,8,16,128]{4,3,2,1,0:T(8,128)} %bitcast.2.refs_2_.up, ...), custom_call_target="tpu_custom_call" | custom-call | flops 1 | bytes 1 | tf_op jit(solution)/shard_map/pallas_call | solution.py:447
  47.8 1.5 %collective-permute-start.11 = (f32[12,6,16,128]{3,2,1,0:T(8,128)}, f32[12,6,16,128]{3,2,1,0:T(8,128)S(1)}, u32[]{:S(2)}, u32[]{:S(2)}) collective-permute-start(f32[12,6,16,128]{3,2,1,0:T(8,128)} %bitcast.35), channel_id=1, source_target_pairs={{0,16},{16,32},{32,48},{48,0},{1,17},{17,33},{33,49},{49,1},{2,18}... | collective-permute-start | bytes 1769480 | tf_op jit(solution)/shard_map/ppermute | solution.py:357
  49.8 1.6 %shard_map.73 = (f32[4,6,16,128]{3,2,1,0:T(8,128)S(1)}, f32[4,6,16,128]{3,2,1,0:T(8,128)S(1)}) custom-call(s32[2]{0:T(128)S(1)} %copy-done.9, f32[2,6,8,16,128]{4,3,2,1,0:T(8,128)} %bitcast.24, f32[2,6,8,16,128]{4,3,2,1,0:T(8,128)} %bitcast.2.refs_2_.up, f32[2,6,8,16,128]{4,3,2,1,0:T(8,128)} %bitcast.3.refs_3_.down, ...), custom_call_target="tpu_custom_call" | custom-call | flops 1 | bytes 1 | tf_op jit(solution)/shard_map/pallas_call | solution.py:467
  53.4 4.6 %collective-permute-done.8 = f32[24,1536]{1,0:T(8,128)S(1)} collective-permute-done((f32[24,1536]{1,0:T(8,128)S(1)}, f32[24,1536]{1,0:T(8,128)S(1)}, u32[]{:S(2)}, u32[]{:S(2)}) %collective-permute-start.8) | collective-permute-done | bytes 147488 | tf_op jit(solution)/shard_map/ppermute | solution.py:427
  58.6 5.9 %collective-permute-start.9 = (f32[24,1536]{1,0:T(8,128)S(1)}, f32[24,1536]{1,0:T(8,128)S(1)}, u32[]{:S(2)}, u32[]{:S(2)}) collective-permute-start(f32[24,1536]{1,0:T(8,128)S(1)} %add.16.one), channel_id=1, source_target_pairs={{0,8},{1,9},{2,10},{3,11},{4,12},{5,13},{6,14},{7,15},{8,0},{9,1},... | collective-permute-start | bytes 442376 | tf_op jit(solution)/shard_map/ppermute | solution.py:493
  64.5 4.7 %collective-permute-done.9.two.refs_8_ = f32[24,1536]{1,0:T(8,128)S(1)} collective-permute-done((f32[24,1536]{1,0:T(8,128)S(1)}, f32[24,1536]{1,0:T(8,128)S(1)}, u32[]{:S(2)}, u32[]{:S(2)}) %collective-permute-start.9) | collective-permute-done | bytes 147488 | tf_op jit(solution)/shard_map/ppermute | solution.py:493
  69.2 2.1 %shard_map.76 = (f32[2,6,2,16,128]{4,3,2,1,0:T(8,128)}, f32[2,6,2,16,128]{4,3,2,1,0:T(8,128)}, f32[2,6,2,16,128]{4,3,2,1,0:T(8,128)}, f32[2,6,2,16,128]{4,3,2,1,0:T(8,128)}) custom-call(f32[1]{0:T(128)S(6)} %div.4.refs_0_, f32[2,6,8,16,128]{4,3,2,1,0:T(8,128)} %bitcast.25, f32[2,6,8,16,128]{4,3,2,1,0:T(8,128)} %bitcast.2.refs_2_.up, ...), custom_call_target="tpu_custom_call" | custom-call | flops 1 | bytes 1 | tf_op jit(solution)/shard_map/pallas_call | solution.py:447
  71.3 1.9 %collective-permute-start.15 = (f32[12,2,16,128]{3,2,1,0:T(8,128)}, f32[12,2,16,128]{3,2,1,0:T(8,128)S(1)}, u32[]{:S(2)}, u32[]{:S(2)}) collective-permute-start(f32[12,2,16,128]{3,2,1,0:T(8,128)} %bitcast.39), channel_id=1, source_target_pairs={{0,48},{16,0},{32,16},{48,32},{1,49},{17,1},{33,17},{49,33},{2,50}... | collective-permute-start | bytes 589832 | tf_op jit(solution)/shard_map/ppermute | solution.py:357
  73.2 2.0 %collective-permute-start.17 = (f32[12,2,16,128]{3,2,1,0:T(8,128)}, f32[12,2,16,128]{3,2,1,0:T(8,128)S(1)}, u32[]{:S(2)}, u32[]{:S(2)}) collective-permute-start(f32[12,2,16,128]{3,2,1,0:T(8,128)} %bitcast.37), channel_id=1, source_target_pairs={{0,32},{16,48},{32,0},{48,16},{1,33},{17,49},{33,1},{49,17},{2,34}... | collective-permute-start | bytes 589832 | tf_op jit(solution)/shard_map/ppermute | solution.py:357
  76.2 5.8 %shard_map.77 = (f32[12,8,64,128]{3,2,1,0:T(8,128)}, f32[12,8,64,128]{3,2,1,0:T(8,128)}) custom-call(bf16[64,192]{1,0:T(8,128)(2,1)S(1)} %copy-done.6, f32[8,12,8,128]{3,2,1,0:T(8,128)S(1)} %shard_map.75.edge, f32[12,8,64,128]{3,2,1,0:T(8,128)S(1)} %bitcast.21, f32[12,6,64,128]{3,2,1,0:T(8,128)} %get-tuple-element.30.refs_5_.pre, ...), custom_call_target="tpu_custom_call" | custom-call | flops 1 | bytes 1 | tf_op jit(solution)/shard_map/pallas_call | solution.py:521
  82.0 3.6 %collective-permute-done.16.rest_2_ = f32[12,2,16,128]{3,2,1,0:T(8,128)S(1)} collective-permute-done((f32[12,2,16,128]{3,2,1,0:T(8,128)}, f32[12,2,16,128]{3,2,1,0:T(8,128)S(1)}, u32[]{:S(2)}, u32[]{:S(2)}) %collective-permute-start.16) | collective-permute-done | bytes 196640 | tf_op jit(solution)/shard_map/ppermute | solution.py:357
  85.6 2.4 %shard_map.78 = (f32[12,8,64,128]{3,2,1,0:T(8,128)}, f32[12,8,64,128]{3,2,1,0:T(8,128)}) custom-call(bf16[64,192]{1,0:T(8,128)(2,1)S(1)} %copy-done.6, f32[8,12,8,128]{3,2,1,0:T(8,128)S(1)} %shard_map.75.edge, f32[12,8,64,128]{3,2,1,0:T(8,128)S(1)} %bitcast.22, f32[12,2,64,128]{3,2,1,0:T(8,128)S(1)} %copy-done.4, ...), custom_call_target="tpu_custom_call", output_to_operand_aliasing={{0}: (8, {}), {1}: (9, {})} | custom-call | flops 1 | bytes 1 | tf_op jit(solution)/shard_map/pallas_call | solution.py:521
  (49 shorter events, 10.6 us)
Async XLA Ops:
  4.2 34.3 %collective-permute-start.3 = (f32[12,8,16,128]{3,2,1,0:T(8,128)}, f32[12,8,16,128]{3,2,1,0:T(8,128)}, u32[]{:S(2)}, u32[]{:S(2)}) collective-permute-start(f32[12,8,16,128]{3,2,1,0:T(8,128)} %get-tuple-element.26), channel_id=1, source_target_pairs={{0,48},{16,0},{32,16},{48,32},{1,49},{17,1},{33,17},{49,33},{2,50}... | collective-permute-start | bytes 2359304 | tf_op jit(solution)/shard_map/ppermute | solution.py:357
  6.8 31.8 %collective-permute-start.5 = (f32[12,8,16,128]{3,2,1,0:T(8,128)}, f32[12,8,16,128]{3,2,1,0:T(8,128)}, u32[]{:S(2)}, u32[]{:S(2)}) collective-permute-start(f32[12,8,16,128]{3,2,1,0:T(8,128)} %get-tuple-element.27), channel_id=1, source_target_pairs={{0,32},{16,48},{32,0},{48,16},{1,33},{17,49},{33,1},{49,17},{2,34}... | collective-permute-start | bytes 2359304 | tf_op jit(solution)/shard_map/ppermute | solution.py:357
  7.3 37.6 %collective-permute-start.4 = (f32[12,8,16,128]{3,2,1,0:T(8,128)}, f32[12,8,16,128]{3,2,1,0:T(8,128)}, u32[]{:S(2)}, u32[]{:S(2)}) collective-permute-start(f32[12,8,16,128]{3,2,1,0:T(8,128)} %get-tuple-element.24.after), channel_id=1, source_target_pairs={{0,16},{16,32},{32,48},{48,0},{1,17},{17,33},{33,49},{49,1},{2,18}... | collective-permute-start | bytes 2359304 | tf_op jit(solution)/shard_map/ppermute | solution.py:357
  9.6 23.4 %copy-start.1 = (f32[1,2,6,8,64,128]{5,4,3,2,1,0:T(8,128)S(1)}, f32[1,2,6,8,64,128]{5,4,3,2,1,0:T(8,128)}, u32[]{:S(2)}) copy-start(f32[1,2,6,8,64,128]{5,4,3,2,1,0:T(8,128)} %param.5) | copy-start | bytes 9437188
  9.6 23.4 %copy-start.3 = (f32[1,8,64,128]{3,2,1,0:T(8,128)S(1)}, f32[1,8,64,128]{3,2,1,0:T(8,128)}, u32[]{:S(2)}) copy-start(f32[1,8,64,128]{3,2,1,0:T(8,128)} %param.6) | copy-start | bytes 786436
  9.6 9.1 %collective-permute-start.1 = (f32[24,1536]{1,0:T(8,128)S(1)}, f32[24,1536]{1,0:T(8,128)S(1)}, u32[]{:S(2)}, u32[]{:S(2)}) collective-permute-start(f32[24,1536]{1,0:T(8,128)S(1)} %shard_map.69), channel_id=1, source_target_pairs={{0,65},{1,64},{2,67},{3,66},{4,69},{5,68},{6,71},{7,70},{8,73},{9,... | collective-permute-start | bytes 442376 | tf_op jit(solution)/shard_map/ppermute | solution.py:429
  13.9 7.5 %collective-permute-start = (f32[24,1536]{1,0:T(8,128)S(1)}, f32[24,1536]{1,0:T(8,128)S(1)}, u32[]{:S(2)}, u32[]{:S(2)}) collective-permute-start(f32[24,1536]{1,0:T(8,128)S(1)} %shard_map.69), channel_id=1, source_target_pairs={{0,64},{1,65},{2,66},{3,67},{4,68},{5,69},{6,70},{7,71},{8,72},{9,... | collective-permute-start | bytes 442376 | tf_op jit(solution)/shard_map/ppermute | solution.py:429
  18.7 6.6 %collective-permute-start.6 = (f32[12,64,128]{2,1,0:T(8,128)S(1)}, f32[12,64,128]{2,1,0:T(8,128)S(1)}, u32[]{:S(2)}, u32[]{:S(2)}) collective-permute-start(f32[12,64,128]{2,1,0:T(8,128)S(1)} %get-tuple-element.28), channel_id=1, source_target_pairs={{0,1},{1,2},{2,3},{3,4},{4,5},{5,6},{6,7},{7,8},{8,9},{9,10},{10,1... | collective-permute-start | bytes 1179656 | tf_op jit(solution)/shard_map/ppermute | solution.py:378
  21.5 11.5 %collective-permute-start.7 = (f32[12,64,128]{2,1,0:T(8,128)}, f32[12,64,128]{2,1,0:T(8,128)}, u32[]{:S(2)}, u32[]{:S(2)}) collective-permute-start(f32[12,64,128]{2,1,0:T(8,128)} %get-tuple-element.29), channel_id=1, source_target_pairs={{1,0},{2,1},{3,2},{4,3},{5,4},{6,5},{7,6},{8,7},{9,8},{10,9},{11,1... | collective-permute-start | bytes 1179656 | tf_op jit(solution)/shard_map/ppermute | solution.py:379
  26.1 12.5 %collective-permute-start.2 = (f32[24,1536]{1,0:T(8,128)}, f32[24,1536]{1,0:T(8,128)S(1)}, u32[]{:S(2)}, u32[]{:S(2)}) collective-permute-start(f32[24,1536]{1,0:T(8,128)} %add.13.one), channel_id=1, source_target_pairs={{0,2},{1,3},{2,0},{3,1},{4,6},{5,7},{6,4},{7,5},{8,10},{9,11},{10,... | collective-permute-start | bytes 442376 | tf_op jit(solution)/shard_map/ppermute | solution.py:431
  38.5 11.2 %copy-start.9 = (s32[2]{0:T(128)S(1)}, s32[2]{0:T(128)}, u32[]{:S(2)}) copy-start(s32[2]{0:T(128)} %counts.1) | copy-start | bytes 28
  47.8 25.4 %collective-permute-start.10 = (f32[12,6,16,128]{3,2,1,0:T(8,128)}, f32[12,6,16,128]{3,2,1,0:T(8,128)S(1)}, u32[]{:S(2)}, u32[]{:S(2)}) collective-permute-start(f32[12,6,16,128]{3,2,1,0:T(8,128)} %bitcast.36), channel_id=1, source_target_pairs={{0,48},{16,0},{32,16},{48,32},{1,49},{17,1},{33,17},{49,33},{2,50}... | collective-permute-start | bytes 1769480 | tf_op jit(solution)/shard_map/ppermute | solution.py:357
  47.8 27.5 %collective-permute-start.11 = (f32[12,6,16,128]{3,2,1,0:T(8,128)}, f32[12,6,16,128]{3,2,1,0:T(8,128)S(1)}, u32[]{:S(2)}, u32[]{:S(2)}) collective-permute-start(f32[12,6,16,128]{3,2,1,0:T(8,128)} %bitcast.35), channel_id=1, source_target_pairs={{0,16},{16,32},{32,48},{48,0},{1,17},{17,33},{33,49},{49,1},{2,18}... | collective-permute-start | bytes 1769480 | tf_op jit(solution)/shard_map/ppermute | solution.py:357
  49.3 26.0 %collective-permute-start.12 = (f32[12,6,16,128]{3,2,1,0:T(8,128)}, f32[12,6,16,128]{3,2,1,0:T(8,128)S(1)}, u32[]{:S(2)}, u32[]{:S(2)}) collective-permute-start(f32[12,6,16,128]{3,2,1,0:T(8,128)} %bitcast.34), channel_id=1, source_target_pairs={{0,32},{16,48},{32,0},{48,16},{1,33},{17,49},{33,1},{49,17},{2,34}... | collective-permute-start | bytes 1769480 | tf_op jit(solution)/shard_map/ppermute | solution.py:357
  51.4 23.9 %copy-start.8 = (s32[8]{0:T(128)S(1)}, s32[8]{0:T(128)}, u32[]{:S(2)}) copy-start(s32[8]{0:T(128)} %orders.3) | copy-start | bytes 100
  52.3 5.6 %collective-permute-start.8 = (f32[24,1536]{1,0:T(8,128)S(1)}, f32[24,1536]{1,0:T(8,128)S(1)}, u32[]{:S(2)}, u32[]{:S(2)}) collective-permute-start(f32[24,1536]{1,0:T(8,128)S(1)} %shard_map.74), channel_id=1, source_target_pairs={{0,4},{1,5},{2,6},{3,7},{4,0},{5,1},{6,2},{7,3},{8,12},{9,13},{10,... | collective-permute-start | bytes 442376 | tf_op jit(solution)/shard_map/ppermute | solution.py:427
  52.7 5.9 %collective-permute-start.14 = (f32[4,6,16,128]{3,2,1,0:T(8,128)S(1)}, f32[4,6,16,128]{3,2,1,0:T(8,128)S(1)}, u32[]{:S(2)}, u32[]{:S(2)}) collective-permute-start(f32[4,6,16,128]{3,2,1,0:T(8,128)S(1)} %get-tuple-element.37), channel_id=1, source_target_pairs={{15,0},{0,15},{31,16},{16,31},{47,32},{32,47},{63,48},{48,63},{79,... | collective-permute-start | bytes 589832 | tf_op jit(solution)/shard_map/ppermute | solution.py:481
  57.9 6.6 %collective-permute-start.13 = (f32[4,6,16,128]{3,2,1,0:T(8,128)S(1)}, f32[4,6,16,128]{3,2,1,0:T(8,128)S(1)}, u32[]{:S(2)}, u32[]{:S(2)}) collective-permute-start(f32[4,6,16,128]{3,2,1,0:T(8,128)S(1)} %get-tuple-element.32.after), channel_id=1, source_target_pairs={{15,0},{0,15},{31,16},{16,31},{47,32},{32,47},{63,48},{48,63},{79,... | collective-permute-start | bytes 589832 | tf_op jit(solution)/shard_map/ppermute | solution.py:481
  58.6 17.5 %copy-start.6 = (bf16[64,192]{1,0:T(8,128)(2,1)S(1)}, bf16[64,192]{1,0:T(8,128)(2,1)}, u32[]{:S(2)}) copy-start(bf16[64,192]{1,0:T(8,128)(2,1)} %constant.16.clone.inverse) | copy-start | bytes 73732
  58.6 10.6 %collective-permute-start.9 = (f32[24,1536]{1,0:T(8,128)S(1)}, f32[24,1536]{1,0:T(8,128)S(1)}, u32[]{:S(2)}, u32[]{:S(2)}) collective-permute-start(f32[24,1536]{1,0:T(8,128)S(1)} %add.16.one), channel_id=1, source_target_pairs={{0,8},{1,9},{2,10},{3,11},{4,12},{5,13},{6,14},{7,15},{8,0},{9,1},... | collective-permute-start | bytes 442376 | tf_op jit(solution)/shard_map/ppermute | solution.py:493
  71.3 10.6 %collective-permute-start.15 = (f32[12,2,16,128]{3,2,1,0:T(8,128)}, f32[12,2,16,128]{3,2,1,0:T(8,128)S(1)}, u32[]{:S(2)}, u32[]{:S(2)}) collective-permute-start(f32[12,2,16,128]{3,2,1,0:T(8,128)} %bitcast.39), channel_id=1, source_target_pairs={{0,48},{16,0},{32,16},{48,32},{1,49},{17,1},{33,17},{49,33},{2,50}... | collective-permute-start | bytes 589832 | tf_op jit(solution)/shard_map/ppermute | solution.py:357
  73.2 12.3 %collective-permute-start.16 = (f32[12,2,16,128]{3,2,1,0:T(8,128)}, f32[12,2,16,128]{3,2,1,0:T(8,128)S(1)}, u32[]{:S(2)}, u32[]{:S(2)}) collective-permute-start(f32[12,2,16,128]{3,2,1,0:T(8,128)} %bitcast.38), channel_id=1, source_target_pairs={{0,16},{16,32},{32,48},{48,0},{1,17},{17,33},{33,49},{49,1},{2,18}... | collective-permute-start | bytes 589832 | tf_op jit(solution)/shard_map/ppermute | solution.py:357
  73.2 12.3 %collective-permute-start.17 = (f32[12,2,16,128]{3,2,1,0:T(8,128)}, f32[12,2,16,128]{3,2,1,0:T(8,128)S(1)}, u32[]{:S(2)}, u32[]{:S(2)}) collective-permute-start(f32[12,2,16,128]{3,2,1,0:T(8,128)} %bitcast.37), channel_id=1, source_target_pairs={{0,32},{16,48},{32,0},{48,16},{1,33},{17,49},{33,1},{49,17},{2,34}... | collective-permute-start | bytes 589832 | tf_op jit(solution)/shard_map/ppermute | solution.py:357
  76.1 9.4 %copy-start.4 = (f32[12,2,64,128]{3,2,1,0:T(8,128)S(1)}, f32[12,2,64,128]{3,2,1,0:T(8,128)}, u32[]{:S(2)}) copy-start(f32[12,2,64,128]{3,2,1,0:T(8,128)} %get-tuple-element.36.pre) | copy-start | bytes 2359300
  (5 other events, 25.7 us)
